TPU v7x, 512 devices: a whole 4x8x8 slice. The times are simulated.
512 devices in a mesh: dp: 32 (over z, x), tensor: 16 (over y, core).
Axes of the slice: x: 4, y: 8, z: 8, core: 2. Of those that a mesh axis runs over, the one named last changes fastest.
Arguments:
- tokens: bfloat16 [12288, 1792], P('dp', 'tensor'), may hold values from -6 to 6
- cotangent: bfloat16 [12288, 1792], P('dp', 'tensor'), may hold values from -6 to 6
- gate_weight: bfloat16 [1792, 8192], P('dp', 'tensor'), may hold values from -0.125 to 0.125
- up_weight: bfloat16 [1792, 8192], P('dp', 'tensor'), may hold values from -0.125 to 0.125
- down_weight: bfloat16 [8192, 1792], P('tensor', 'dp'), may hold values from -0.0625 to 0.0625
- error_buffer: bfloat16 [32, 8192, 1792], P('dp', 'tensor'), may hold values from -803.4326 to 803.4326
- q_init: float32 [8, 1792], replicated, may hold values from -6 to 6
Outputs:
- grad_tokens: bfloat16 [12288, 1792], P('dp', 'tensor')
- new_error: bfloat16 [32, 8192, 1792], P('dp', 'tensor')
- q_avg: float32 [8, 1792], replicated
All inputs are finite; a program needn't handle non-finite values.
Results may differ from a plain program's by a relative error of at most 0.0049.
Values may be sent and summed in bfloat16 or wider, within the bound.
No kernel may reach another device: no remote copies, remote signals or barrier semaphores. Data moves between devices by JAX's collectives and lax.ppermute only.
A program may use at most 64 MiB of HBM per device.

v0:
```python
import math

import jax
import jax.numpy as jnp
from jax import lax
from jax.sharding import PartitionSpec as P

cubic_term = 0.044715
tanh_scale = math.sqrt(2.0 / math.pi)
highest = lax.Precision.HIGHEST


def gelu_parts(values):
    inner = tanh_scale * (values + cubic_term * values * values * values)
    tanh_val = jnp.tanh(inner)
    active = 0.5 * values * (1.0 + tanh_val)
    slope = 0.5 * (1.0 + tanh_val) + 0.5 * values * (1.0 - tanh_val * tanh_val) * tanh_scale * (
        1.0 + 3.0 * cubic_term * values * values
    )
    return (active, slope)


def times_trans(left, right):
    return lax.dot_general(
        left, right, (((1,), (1,)), ((), ())), preferred_element_type=jnp.float32
    )


def per_device(tokens, cotangent, gate_weight, up_weight, down_weight, error_buffer, q_init):
    inputs, upstream = (
        lax.all_gather(tokens, "tensor", axis=1, tiled=True),
        lax.all_gather(cotangent, "tensor", axis=1, tiled=True),
    )
    pieces = (
        lax.all_gather(gate_weight, "dp", axis=0, tiled=True),
        lax.all_gather(up_weight, "dp", axis=0, tiled=True),
    )
    columns = inputs
    gate = jnp.dot(columns, pieces[0], preferred_element_type=jnp.float32)
    up_val = jnp.dot(columns, pieces[1], preferred_element_type=jnp.float32)
    active, slope = gelu_parts(gate)
    hidden = (active * up_val).astype(jnp.bfloat16)
    columns = upstream
    d_hidden = times_trans(columns, lax.all_gather(down_weight, "dp", axis=1, tiled=True))
    d_gate = (d_hidden * up_val * slope).astype(jnp.bfloat16)
    d_up = (d_hidden * active).astype(jnp.bfloat16)
    pieces = (
        lax.all_gather(gate_weight, "dp", axis=0, tiled=True),
        lax.all_gather(up_weight, "dp", axis=0, tiled=True),
    )
    block = times_trans(d_gate, pieces[0]) + times_trans(d_up, pieces[1])
    grad_tokens = lax.psum_scatter(block, "tensor", scatter_dimension=1, tiled=True).astype(
        jnp.bfloat16
    )
    local_grad = lax.dot_general(
        hidden, upstream, (((0,), (0,)), ((), ())), preferred_element_type=jnp.float32
    )
    merged = local_grad + error_buffer[0].astype(jnp.float32)
    p_part = lax.dot_general(
        q_init,
        merged,
        (((1,), (1,)), ((), ())),
        precision=highest,
        preferred_element_type=jnp.float32,
    )
    p_sum = lax.psum(p_part, "dp")
    row_list = [p_sum[position] for position in range(p_sum.shape[0])]
    for position in range(len(row_list)):
        remaining = jnp.stack(row_list[position:])
        products = lax.psum(jnp.dot(remaining, row_list[position], precision=highest), "tensor")
        length = jnp.sqrt(products[0])
        unit_row = row_list[position] / length
        for later in range(position + 1, len(row_list)):
            row_list[later] = row_list[later] - products[later - position] / length * unit_row
        row_list[position] = unit_row
    p_orth = jnp.stack(row_list)
    q_part = jnp.dot(p_orth, merged, precision=highest, preferred_element_type=jnp.float32)
    q_avg = lax.psum(q_part, ("dp", "tensor")) / lax.axis_size("dp")
    approx = lax.dot_general(
        p_orth,
        q_avg,
        (((0,), (0,)), ((), ())),
        precision=highest,
        preferred_element_type=jnp.float32,
    )
    new_error = (merged - approx).astype(jnp.bfloat16)[None]
    return (grad_tokens, new_error, q_avg)


def solution(mesh):
    return jax.shard_map(
        per_device,
        mesh=mesh,
        in_specs=(
            P("dp", "tensor"),
            P("dp", "tensor"),
            P("dp", "tensor"),
            P("dp", "tensor"),
            P("tensor", "dp"),
            P("dp", "tensor", None),
            P(),
        ),
        out_specs=(P("dp", "tensor"), P("dp", "tensor", None), P()),
        check_vma=False,
    )
```

profile of v0, /device:TPU:1, one launch (start us, length us, event | category | flops | bytes accessed | tf_op | source)
XLA Modules:
  0.0 757.3 jit_solution(1330837135865439006)
XLA Ops:
  7.2 0.7 all-gather.10.cloned.1.call-update
  7.9 0.0 all-gather.14.cloned.1.call-start
  8.0 0.7 all-gather.14.cloned.1.call-update
  8.7 0.7 all-gather.12.cloned.1.call-update
  9.4 0.5 all-gather.6.cloned.1.call-update
  10.0 0.5 all-gather.8.cloned.1.call-update
  10.6 0.0 reduce-scatter.2.cloned.1.call-start
  10.6 46.7 %all-gather.10.cloned.1.call-done = bf16[384,1792]{0,1:T(8,128)(2,1)} async-done(((bf16[384,112]{0,1:T(8,128)(2,1)}), bf16[384,1792]{0,1:T(8,128)(2,1)}) %all-gather.10.cloned.1.call-update) | async-done | bytes 1376272 | tf_op jit(solution)/shard_map/all_gather | solution.py:31
  57.3 81.4 %all-gather.14.cloned.1.call-done = bf16[1792,512]{1,0:T(8,128)(2,1)} async-done(((bf16[56,512]{1,0:T(8,128)(2,1)}), bf16[1792,512]{1,0:T(8,128)(2,1)}) %all-gather.14.cloned.1.call-update) | async-done | bytes 1835024 | tf_op jit(solution)/shard_map/all_gather | solution.py:35
  138.8 2.8 fusion.55
  141.6 80.8 %all-gather.12.cloned.1.call-done = bf16[1792,512]{1,0:T(8,128)(2,1)} async-done(((bf16[56,512]{1,0:T(8,128)(2,1)}), bf16[1792,512]{1,0:T(8,128)(2,1)}) %all-gather.12.cloned.1.call-update) | async-done | bytes 1835024 | tf_op jit(solution)/shard_map/all_gather | solution.py:36
  222.4 2.4 fusion.54
  224.8 42.1 %all-gather.6.cloned.1.call-done = bf16[384,1792]{0,1:T(8,128)(2,1)} async-done(((bf16[384,112]{0,1:T(8,128)(2,1)}), bf16[384,1792]{0,1:T(8,128)(2,1)}) %all-gather.6.cloned.1.call-update) | async-done | bytes 1376272 | tf_op jit(solution)/shard_map/all_gather | solution.py:32
  266.8 3.2 convert_add_fusion
  270.1 1.8 copy-done.1
  271.8 3.2 convolution_bitcast_fusion
  275.0 116.5 %psum.70 = f32[8,512]{1,0:T(8,128)S(1)} all-reduce(f32[8,512]{1,0:T(8,128)S(1)} %convolution_bitcast_fusion), channel_id=1, replica_groups=mesh['dp'=32,'tensor'=16] {'dp'}, use_global_device_ids=true, to_apply=%region_1.0 | all-reduce | flops 4096 | bytes 32768 | tf_op jit(solution)/shard_map/psum | solution.py:66
  391.5 0.1 convolution_bitcast_fusion.7
  391.6 50.6 %psum.71 = f32[8]{0:T(128)S(1)} all-reduce(f32[8]{0:T(128)S(1)} %convolution_bitcast_fusion.7), channel_id=1, replica_groups=mesh['dp'=32,'tensor'=16] {'tensor'}, use_global_device_ids=true, to_apply=%region_2.0 | all-reduce | flops 8 | bytes 64 | tf_op jit(solution)/shard_map/psum | solution.py:70
  442.2 0.6 fusion.52
  448.1 0.1 convolution_bitcast_fusion.6
  448.2 3.0 fusion.53
  451.2 1.3 fusion.8
  452.6 0.1 copy-done.3
  452.7 2.8 convolution_add_fusion
  455.5 23.6 %psum.72 = f32[7]{0:T(128)S(1)} all-reduce(f32[7]{0:T(128)S(1)} %convolution_bitcast_fusion.6), channel_id=1, replica_groups=mesh['dp'=32,'tensor'=16] {'tensor'}, use_global_device_ids=true, to_apply=%region_3.0 | all-reduce | flops 7 | bytes 56 | tf_op jit(solution)/shard_map/psum | solution.py:70
  479.1 0.7 fusion.51
  484.4 0.1 convolution_bitcast_fusion.5
  484.5 23.5 %psum.73 = f32[6]{0:T(128)S(1)} all-reduce(f32[6]{0:T(128)S(1)} %convolution_bitcast_fusion.5), channel_id=1, replica_groups=mesh['dp'=32,'tensor'=16] {'tensor'}, use_global_device_ids=true, to_apply=%region_4.0 | all-reduce | flops 6 | bytes 48 | tf_op jit(solution)/shard_map/psum | solution.py:70
  508.1 0.7 fusion.50
  512.8 0.1 convolution_bitcast_fusion.4
  512.9 23.6 %psum.74 = f32[5]{0:T(128)S(1)} all-reduce(f32[5]{0:T(128)S(1)} %convolution_bitcast_fusion.4), channel_id=1, replica_groups=mesh['dp'=32,'tensor'=16] {'tensor'}, use_global_device_ids=true, to_apply=%region_5.0 | all-reduce | flops 5 | bytes 40 | tf_op jit(solution)/shard_map/psum | solution.py:70
  536.5 0.6 fusion.49
  540.5 0.1 convolution_bitcast_fusion.3
  540.6 23.5 %psum.75 = f32[4]{0:T(128)S(1)} all-reduce(f32[4]{0:T(128)S(1)} %convolution_bitcast_fusion.3), channel_id=1, replica_groups=mesh['dp'=32,'tensor'=16] {'tensor'}, use_global_device_ids=true, to_apply=%region_6.0 | all-reduce | flops 4 | bytes 32 | tf_op jit(solution)/shard_map/psum | solution.py:70
  564.1 0.6 fusion.48
  567.4 0.1 convolution_bitcast_fusion.2
  567.6 23.5 %psum.76 = f32[3]{0:T(128)S(1)} all-reduce(f32[3]{0:T(128)S(1)} %convolution_bitcast_fusion.2), channel_id=1, replica_groups=mesh['dp'=32,'tensor'=16] {'tensor'}, use_global_device_ids=true, to_apply=%region_7.0 | all-reduce | flops 3 | bytes 24 | tf_op jit(solution)/shard_map/psum | solution.py:70
  591.1 0.6 fusion.47
  593.8 0.1 convolution_bitcast_fusion.1
  593.9 23.5 %psum.77 = f32[2]{0:T(128)S(1)} all-reduce(f32[2]{0:T(128)S(1)} %convolution_bitcast_fusion.1), channel_id=1, replica_groups=mesh['dp'=32,'tensor'=16] {'tensor'}, use_global_device_ids=true, to_apply=%region_8.0 | all-reduce | flops 2 | bytes 16 | tf_op jit(solution)/shard_map/psum | solution.py:70
  617.5 0.6 fusion.46
  619.4 0.6 multiply_reduce_fusion
  620.0 24.3 %psum.78 = f32[1]{0:T(128)} all-reduce(f32[1]{0:T(128)} %bitcast.59), channel_id=1, replica_groups=mesh['dp'=32,'tensor'=16] {'tensor'}, use_global_device_ids=true, to_apply=%region_9.0 | all-reduce | flops 1 | bytes 8 | tf_op jit(solution)/shard_map/psum | solution.py:70
  645.1 3.8 fusion.56
  648.9 94.3 %psum.79 = f32[8,1792]{1,0:T(8,128)S(1)} all-reduce(f32[8,1792]{1,0:T(8,128)S(1)} %fusion.56), channel_id=1, replica_groups=mesh['dp'=32,'tensor'=16] {'dp','tensor'}, use_global_device_ids=true, to_apply=%region_10.0 | all-reduce | flops 14336 | bytes 114688 | tf_op jit(solution)/shard_map/psum | solution.py:78
  743.2 5.7 fusion
  748.9 1.6 convert_element_type.23
  (42 shorter events, 0.6 us)
Async XLA Ops:
  7.2 264.7 %copy-start = (f32[8,1792]{1,0:T(8,128)S(1)}, f32[8,1792]{1,0:T(8,128)}, u32[]{:S(2)}) copy-start(f32[8,1792]{1,0:T(8,128)} %param.13) | copy-start | bytes 172036
  7.2 50.2 %all-gather.10.cloned.1.call-start = ((), (), s32[]{:S(2)}) async-start(), calls=%async_computation.3 | async-start | bytes 1462272 | tf_op jit(solution)/shard_map/all_gather | solution.py:31
  7.9 130.8 %all-gather.14.cloned.1.call-start = ((), (), s32[]{:S(2)}) async-start(), calls=%async_computation.5 | async-start | bytes 1892352 | tf_op jit(solution)/shard_map/all_gather | solution.py:35
  8.7 213.7 %all-gather.12.cloned.1.call-start = ((), (), s32[]{:S(2)}) async-start(), calls=%async_computation.4 | async-start | bytes 1892352 | tf_op jit(solution)/shard_map/all_gather | solution.py:36
  9.4 257.4 %all-gather.6.cloned.1.call-start = ((), (), s32[]{:S(2)}) async-start(), calls=%async_computation.1 | async-start | bytes 1462272 | tf_op jit(solution)/shard_map/all_gather | solution.py:32
  10.0 438.3 %all-gather.8.cloned.1.call-start = ((), (), s32[]{:S(2)}) async-start(), calls=%async_computation.2 | async-start | bytes 1892352 | tf_op jit(solution)/shard_map/all_gather | solution.py:44
  10.6 738.4 %reduce-scatter.2.cloned.1.call-start = ((), (), s32[]{:S(2)}) async-start(), calls=%async_computation.6 | async-start | bytes 2924544 | tf_op jit(solution)/shard_map/reduce_scatter | solution.py:52
  57.3 165.0 %copy-start.4 = (bf16[384,1792]{0,1:T(8,128)(2,1)S(1)}, bf16[384,1792]{0,1:T(8,128)(2,1)}, u32[]{:S(2)}) copy-start(bf16[384,1792]{0,1:T(8,128)(2,1)} %all-gather.10.cloned.1.call-done) | copy-start | bytes 4128772
  270.1 1.8 copy-start.1
  448.2 3.0 copy-start.2
  451.2 1.5 copy-start.3
  743.2 5.8 copy-start.5
Sparse Core Ops, SparseCore 0:
  10.1 47.1 all-gather.9
  60.5 78.2 all-gather.13
  141.9 80.3 all-gather.11
  224.3 42.4 all-gather.5
  269.8 78.2 all-gather.7
  455.6 53.7 reduce-scatter.1
where the time goes:
time: 758 us; the launch traced here: 757 us
  blocking collectives  427 us (56%)
  waiting for transfers between devices  254 us (34%)
  between operations  37.9 us (5%)
  matrix products  29.2 us (4%)
    psum x8, blocking collectives, per_device(): lax.psum(jnp.dot(remaining, row_list[position], precision=highest), 'tens...  216 us
    psum x1, blocking collectives, per_device(): p_sum = lax.psum(p_part, 'dp')  116 us
    psum x1, blocking collectives, per_device(): q_avg = lax.psum(q_part, ('dp', 'tensor')) / lax.axis_size('dp')  94.3 us
    all_gather x1, waiting for transfers between devices, per_device(): lax.all_gather(gate_weight, 'dp', axis=0, tiled=True)  81.4 us
    all_gather x1, waiting for transfers between devices, per_device(): lax.all_gather(up_weight, 'dp', axis=0, tiled=True)  80.8 us
    all_gather x1, waiting for transfers between devices, per_device(): lax.all_gather(tokens, 'tensor', axis=1, tiled=True)  46.7 us
    all_gather x1, waiting for transfers between devices, per_device(): lax.all_gather(cotangent, 'tensor', axis=1, tiled=True)  42.1 us
  transfers between devices with their start and end apart: 6, of which 4 were waited for; matrix products, arithmetic and copies ran while one was open for 4% of the time, Pallas kernels for 0%

commit v1 on v0

v1 whole, which is shorter than its diff:
```python
import math

import jax
import jax.numpy as jnp
from jax import lax
from jax.experimental import pallas as pl
from jax.experimental.pallas import tpu as pltpu
from jax.sharding import Mesh, PartitionSpec as P

cubic_term = 0.044715
tanh_scale = math.sqrt(2.0 / math.pi)
bf16 = jnp.bfloat16
f32 = jnp.float32

Z, X, Y, C = 8, 4, 8, 2
SIZE = {"z": Z, "x": X, "y": Y, "c": C}
RANK = 8
LANES = 128


def gelu_parts(values):
    inner = tanh_scale * (values + cubic_term * values * values * values)
    tanh_val = jnp.tanh(inner)
    active = 0.5 * values * (1.0 + tanh_val)
    slope = 0.5 * (1.0 + tanh_val) + 0.5 * values * (1.0 - tanh_val * tanh_val) * tanh_scale * (
        1.0 + 3.0 * cubic_term * values * values
    )
    return (active, slope)


def contract(left, right, dim_left, dim_right):
    return lax.dot_general(
        left, right, (((dim_left,), (dim_right,)), ((), ())), preferred_element_type=f32
    )


def shift(value, axis, step):
    n = SIZE[axis]
    return lax.ppermute(value, axis, [(i, (i + step) % n) for i in range(n)])


def swap(stacked, axes):
    return lax.all_to_all(stacked, axes, 0, 0, tiled=True)


def gather(value, axes):
    n = math.prod(SIZE[a] for a in axes)
    return swap(jnp.broadcast_to(value[None], (n,) + value.shape), axes)


def pieces(value):
    first = lax.reduce_precision(value, 8, 7)
    rest = value - first
    second = lax.reduce_precision(rest, 8, 7)
    third = rest - second
    return first.astype(bf16), second.astype(bf16), third.astype(bf16)


def stack3(value):
    return jnp.concatenate(pieces(value), axis=0)


def fold3(value):
    n = value.shape[0] // 3
    return value[:n] + (value[n : 2 * n] + value[2 * n :])


def orth_kernel(mine, parts, orth, transform, rows):
    blocks, _, width = parts.shape
    width = width - LANES
    for t in range(blocks):
        rows[:, t * width : (t + 1) * width] = parts[t, :, LANES:]
    number = lax.broadcasted_iota(jnp.int32, (RANK, 1), 0)
    column = lax.broadcasted_iota(jnp.int32, (RANK, LANES), 1)
    trans = jnp.where(column == number, 1.0, 0.0).astype(f32)
    for j in range(RANK):
        whole = rows[...]
        row = whole[j : j + 1, :]
        products = jnp.sum(whole * row, axis=1, keepdims=True)
        length = jnp.sqrt(products[j : j + 1, :])
        unit = row / length
        weight = jnp.where(number > j, products / length, 0.0)
        rows[...] = jnp.where(number == j, unit, whole - weight * unit)
        unit_trans = trans[j : j + 1, :] / length
        trans = jnp.where(number == j, unit_trans, trans - weight * unit_trans)
    transform[...] = trans
    at = pl.multiple_of(mine[0] * width, LANES)
    orth[...] = rows[:, pl.ds(at, width)]


def orthonormal(parts, mine):
    blocks, _, width = parts.shape
    width = width - LANES
    return pl.pallas_call(
        orth_kernel,
        out_shape=(
            jax.ShapeDtypeStruct((RANK, width), f32),
            jax.ShapeDtypeStruct((RANK, LANES), f32),
        ),
        in_specs=[
            pl.BlockSpec(memory_space=pltpu.SMEM),
            pl.BlockSpec(memory_space=pltpu.VMEM),
        ],
        out_specs=(
            pl.BlockSpec(memory_space=pltpu.VMEM),
            pl.BlockSpec(memory_space=pltpu.VMEM),
        ),
        scratch_shapes=[pltpu.VMEM((RANK, blocks * width), f32)],
        compiler_params=pltpu.CompilerParams(vmem_limit_bytes=16 * 1024 * 1024),
    )(mine, parts)


def per_device(tokens, cotangent, gate_weight, up_weight, down_weight, error_buffer, q_init):
    y_at = lax.axis_index("y")
    c_at = lax.axis_index("c")
    errors = error_buffer[0]
    units = gate_weight.shape[1]

    pair = swap(jnp.stack([tokens.T, cotangent.T]), ("c",))
    block = pair.reshape(-1, pair.shape[-1])
    far = shift(block, "y", 4)
    back2 = shift(block, "y", 2)
    fore2 = shift(block, "y", -2)
    both = jnp.stack([block, far])
    back = shift(both, "y", 1)
    fore = shift(both, "y", -1)
    in_turn = jnp.stack([block, fore[0], fore2, back[1], far, fore[1], back2, back[0]])
    twice = jnp.concatenate([in_turn, in_turn], axis=0)
    ordered = lax.dynamic_slice_in_dim(twice, (Y - y_at) % Y, Y, axis=0)
    inputs, upstream = gather(ordered.reshape(-1, block.shape[-1]), ("c",))

    side = gather(jnp.stack([up_weight, down_weight.T]), ("x",))
    up_all = lax.all_gather(side[:, 0].reshape(-1, units), "z", axis=0, tiled=True)
    down_all = lax.all_gather(side[:, 1].reshape(-1, units), "z", axis=0, tiled=True)
    gate_z = gather(gate_weight, ("z",))
    gate_all = gather(gate_z, ("x",)).transpose(1, 0, 2, 3).reshape(-1, units)

    gate = contract(gate_all, inputs, 0, 0)
    up_val = contract(up_all, inputs, 0, 0)
    active, slope = gelu_parts(gate)
    hidden = (active * up_val).astype(bf16)

    q_stack = stack3(q_init)
    cot_q = stack3(fold3(contract(q_stack, upstream, 1, 0)))
    err_q = fold3(contract(q_stack, errors, 1, 1))
    p_part = fold3(contract(cot_q, hidden, 1, 1)) + err_q
    p_sum = jnp.sum(gather(p_part, ("z", "x")), axis=0)

    p_stack = stack3(p_sum)
    hid_p = stack3(fold3(contract(p_stack, hidden, 1, 0)))
    q_part = fold3(contract(p_stack, errors, 1, 0)) + fold3(contract(hid_p, upstream, 1, 1))
    tiles = q_part.reshape(RANK, -1, LANES).transpose(1, 0, 2)
    n_tiles = tiles.shape[0]
    tiles = jnp.concatenate([tiles, jnp.zeros((Y * C - n_tiles,) + tiles.shape[1:], f32)])
    message = jnp.concatenate(
        [tiles, jnp.broadcast_to(p_sum[None], (Y * C,) + p_sum.shape)], axis=2
    )
    parts = swap(message, ("y", "c"))
    q_tile = jnp.sum(parts[:, :, :LANES], axis=0)
    p_orth, trans = orthonormal(parts, (y_at * C + c_at).astype(jnp.int32).reshape(1))
    q_tile = jnp.sum(gather(q_tile, ("z", "x")), axis=0)
    q_tile = jnp.dot(trans[:, :RANK], q_tile, precision=lax.Precision.HIGHEST) / (Z * X)
    q_avg = gather(q_tile, ("y", "c"))[:n_tiles].transpose(1, 0, 2).reshape(RANK, -1)

    p1, p2, p3 = pieces(p_orth)
    q1, q2, q3 = pieces(q_avg)
    approx = contract(
        jnp.concatenate([p1, p1, p2, p2, p1, p3]),
        jnp.concatenate([q1, q2, q1, q2, q3, q1]),
        0,
        0,
    )
    local_grad = contract(hidden, upstream, 1, 1)
    new_error = (local_grad + errors.astype(f32) - approx).astype(bf16)[None]

    d_hidden = contract(down_all, upstream, 0, 0)
    d_gate = (d_hidden * up_val * slope).astype(bf16)
    d_up = (d_hidden * active).astype(bf16)
    grads = contract(gate_all, d_gate, 1, 0) + contract(up_all, d_up, 1, 0)
    grads = grads.reshape(Y, C, -1, grads.shape[-1])
    keep = jnp.where(c_at == 0, grads[:, 0], grads[:, 1])
    give = jnp.where(c_at == 0, grads[:, 1], grads[:, 0])
    chip = keep + shift(give, "c", 1)
    grad_tokens = lax.psum_scatter(chip, "y", scatter_dimension=0, tiled=False)
    return (grad_tokens.astype(bf16).T, new_error, q_avg)


def solution(mesh):
    fine = Mesh(mesh.devices.reshape(Z, X, Y, C), ("z", "x", "y", "c"))
    dp, tensor = ("z", "x"), ("y", "c")
    return jax.shard_map(
        per_device,
        mesh=fine,
        in_specs=(
            P(dp, tensor),
            P(dp, tensor),
            P(dp, tensor),
            P(dp, tensor),
            P(tensor, dp),
            P(dp, tensor, None),
            P(),
        ),
        out_specs=(P(dp, tensor), P(dp, tensor, None), P()),
        check_vma=False,
    )
```

time: 758 us -> 226 us (0.30)
  blocking collectives: 427 us -> 18.4 us
  waiting for transfers between devices: 254 us -> 70.8 us
  starting transfers between devices: 0.23 us -> 59 us
  between operations: 37.9 us -> 14.2 us
  local copies, waits for them, and re-layouts: 6.46 us -> 24 us
    psum x10 -> x0, blocking collectives: 427 us -> none  [the longest x8 216 us: per_device(): lax.psum(jnp.dot(remaining, row_list[position], precision=highest), 'tens...]
    all_gather x5 -> x2, waiting for transfers between devices: 251 us -> 0.02 us  [the longest x1 0.02 us: per_device(): lax.all_gather(side[:, 1].reshape(-1, units), 'z', axis=0, tiled=True)]
    all_to_all x0 -> x7, waiting for transfers between devices: none -> 63 us  [swap(): return lax.all_to_all(stacked, axes, 0, 0, tiled=True)]
    all_to_all x0 -> x7, starting transfers between devices: none -> 41.8 us  [swap(): return lax.all_to_all(stacked, axes, 0, 0, tiled=True)]
    all_to_all x0 -> x2, blocking collectives: none -> 18.4 us  [swap(): return lax.all_to_all(stacked, axes, 0, 0, tiled=True)]
    ppermute x0 -> x6, starting transfers between devices: none -> 16.9 us  [shift(): return lax.ppermute(value, axis, [(i, (i + step) % n) for i in range(n)])]
    unnamed x12 -> x35, local copies, waits for them, and re-layouts: 1.94 us -> 11.6 us
    dot_general x16 -> x14, matrix products: 29.2 us -> 27.4 us  [the longest x13 27.3 us: contract(): lax.dot_general(left, right, (((dim_left,), (dim_right,)), ((), ())), pre...]
  transfers between devices with their start and end apart: 6 -> 16, of which waited for: 4 -> 8; matrix products, arithmetic and copies ran while one was open for 4% -> 25% of each run, Pallas kernels for 0% -> 1%
where the time goes in v1:
time: 226 us; the launch traced here: 225 us
  waiting for transfers between devices  70.8 us (31%)
  starting transfers between devices  59 us (26%)
  matrix products  27.4 us (12%)
  local copies, waits for them, and re-layouts  24 us (11%)
  blocking collectives  18.4 us (8%)
  between operations  14.2 us (6%)
  other arithmetic  9.41 us (4%)
    all_to_all x7, waiting for transfers between devices, swap(): return lax.all_to_all(stacked, axes, 0, 0, tiled=True)  63 us
    all_to_all x7, starting transfers between devices, swap(): return lax.all_to_all(stacked, axes, 0, 0, tiled=True)  41.8 us
    dot_general x13, matrix products, contract(): lax.dot_general(left, right, (((dim_left,), (dim_right,)), ((), ())), pre...  27.3 us
    all_to_all x2, blocking collectives, swap(): return lax.all_to_all(stacked, axes, 0, 0, tiled=True)  18.4 us
    ppermute x6, starting transfers between devices, shift(): return lax.ppermute(value, axis, [(i, (i + step) % n) for i in range(n)])  16.9 us
    unnamed x35, local copies, waits for them, and re-layouts  11.6 us
    ppermute x6, waiting for transfers between devices, shift(): return lax.ppermute(value, axis, [(i, (i + step) % n) for i in range(n)])  7.07 us
    broadcast_in_dim x7, local copies, waits for them, and re-layouts, gather(): return swap(jnp.broadcast_to(value[None], (n,) + value.shape), axes)  5.44 us
  transfers between devices with their start and end apart: 16, of which 8 were waited for; matrix products, arithmetic and copies ran while one was open for 25% of the time, Pallas kernels for 1%

profile of v1, /device:TPU:1, one launch (start us, length us, event | category | flops | bytes accessed | tf_op | source)
XLA Modules:
  0.0 224.7 jit_solution(4416688731103978749)
XLA Ops:
  7.2 1.0 pad_maximum_fusion.1
  8.1 10.4 %all_to_all.45 = bf16[2,112,384]{2,1,0:T(8,128)(2,1)S(1)} all-to-all(bf16[2,112,384]{2,1,0:T(8,128)(2,1)S(1)} %pad_maximum_fusion.1), channel_id=1, replica_groups=mesh['z'=8,'x'=4,'y'=8,'c'=2] {'c'}, dimensions={0} | all-to-all | bytes 344064 | tf_op jit(solution)/shard_map/all_to_all | solution.py:43
  18.5 2.1 collective-permute-start
  20.6 0.9 pad_maximum_fusion.2
  21.4 0.8 broadcast_in_dim.20
  22.2 4.0 %all-to-all-start = ((bf16[4,2,56,512]{3,2,1,0:T(8,128)(2,1)}), bf16[4,2,56,512]{3,2,1,0:T(8,128)(2,1)S(1)}, u32[]{:S(2)}, u32[]{:S(2)}) async-start(bf16[4,2,56,512]{3,2,1,0:T(8,128)(2,1)} %broadcast_in_dim.20), calls=%async_computation | async-start | bytes 917504 | tf_op jit(solution)/shard_map/all_to_all | solution.py:43
  26.3 2.0 collective-permute-start.2
  28.2 4.2 %collective-permute-start.4 = (bf16[224,384]{1,0:T(8,128)(2,1)S(1)}, bf16[224,384]{1,0:T(8,128)(2,1)S(1)}, u32[]{:S(2)}, u32[]{:S(2)}) collective-permute-start(bf16[224,384]{1,0:T(8,128)(2,1)S(1)} %bitcast.106), channel_id=1, source_target_pairs={{0,4},{2,6},{4,8},{6,10},{8,12},{10,14},{12,0},{14,2},{1,5},{3,7},... | collective-permute-start | bytes 516104 | tf_op jit(solution)/shard_map/ppermute | solution.py:39
  32.6 3.2 %collective-permute-start.1 = (bf16[2,224,384]{2,1,0:T(8,128)(2,1)S(1)}, bf16[2,224,384]{2,1,0:T(8,128)(2,1)S(1)}, u32[]{:S(2)}, u32[]{:S(2)}) collective-permute-start(bf16[2,224,384]{2,1,0:T(8,128)(2,1)S(1)} %pad_maximum_fusion), channel_id=1, source_target_pairs={{0,14},{2,0},{4,2},{6,4},{8,6},{10,8},{12,10},{14,12},{1,15},{3,1}... | collective-permute-start | bytes 1032200 | tf_op jit(solution)/shard_map/ppermute | solution.py:39
  36.5 2.1 collective-permute-start.3
  38.6 0.8 fusion.70
  39.5 6.9 %collective-permute-done.1 = bf16[2,224,384]{2,1,0:T(8,128)(2,1)S(1)} collective-permute-done((bf16[2,224,384]{2,1,0:T(8,128)(2,1)S(1)}, bf16[2,224,384]{2,1,0:T(8,128)(2,1)S(1)}, u32[]{:S(2)}, u32[]{:S(2)}) %collective-permute-start.1) | collective-permute-done | bytes 344096 | tf_op jit(solution)/shard_map/ppermute | solution.py:39
  56.7 1.5 constant_dynamic-slice_fusion
  58.5 8.1 %all_to_all.46 = bf16[2,1792,384]{2,1,0:T(8,128)(2,1)S(1)} all-to-all(bf16[2,1792,384]{2,1,0:T(8,128)(2,1)S(1)} %broadcast_in_dim.22), channel_id=1, replica_groups=mesh['z'=8,'x'=4,'y'=8,'c'=2] {'c'}, dimensions={0} | all-to-all | bytes 5505024 | tf_op jit(solution)/shard_map/all_to_all | solution.py:43
  66.5 0.8 broadcast_in_dim.23
  67.4 10.0 %all-to-all-start.3 = ((bf16[8,56,512]{2,1,0:T(8,128)(2,1)}), bf16[8,56,512]{2,1,0:T(8,128)(2,1)S(1)}, u32[]{:S(2)}, u32[]{:S(2)}) async-start(bf16[8,56,512]{2,1,0:T(8,128)(2,1)} %broadcast_in_dim.23), calls=%async_computation.3 | async-start | bytes 917504 | tf_op jit(solution)/shard_map/all_to_all | solution.py:43
  78.2 16.6 %all-to-all-done.3 = bf16[8,56,512]{2,1,0:T(8,128)(2,1)S(1)} async-done(((bf16[8,56,512]{2,1,0:T(8,128)(2,1)}), bf16[8,56,512]{2,1,0:T(8,128)(2,1)S(1)}, u32[]{:S(2)}, u32[]{:S(2)}) %all-to-all-start.3) | async-done | bytes 458784 | tf_op jit(solution)/shard_map/all_to_all | solution.py:43
  94.8 1.4 broadcast_in_dim.24
  96.1 4.4 %all-to-all-start.4 = ((bf16[4,8,56,512]{3,2,1,0:T(8,128)(2,1)}), bf16[4,8,56,512]{3,2,1,0:T(8,128)(2,1)}, u32[]{:S(2)}, u32[]{:S(2)}) async-start(bf16[4,8,56,512]{3,2,1,0:T(8,128)(2,1)} %broadcast_in_dim.24), calls=%async_computation.4 | async-start | bytes 3670016 | tf_op jit(solution)/shard_map/all_to_all | solution.py:43
  100.6 2.1 fusion.3
  103.0 20.3 %all-to-all-done.4 = bf16[4,8,56,512]{3,2,1,0:T(8,128)(2,1)} async-done(((bf16[4,8,56,512]{3,2,1,0:T(8,128)(2,1)}), bf16[4,8,56,512]{3,2,1,0:T(8,128)(2,1)}, u32[]{:S(2)}, u32[]{:S(2)}) %all-to-all-start.4) | async-done | bytes 1835040 | tf_op jit(solution)/shard_map/all_to_all | solution.py:43
  123.4 1.7 copy.29
  125.1 1.2 copy-done.2
  126.3 2.0 convolution_bitcast_fusion.1
  128.4 3.7 %multiply_convert_fusion = (bf16[512,384]{1,0:T(8,128)(2,1)S(1)}, f32[512,384]{1,0:T(8,128)}) fusion(f32[512,384]{1,0:T(8,128)} %convolution_bitcast_fusion.1, bf16[1792,512]{1,0:T(8,128)(2,1)} %all-gather.5.cloned.1.call-done, bf16[2,1792,384]{2,1,0:T(8,128)(2,1)S(1)} %all_to_all.46), kind=kOutput, calls=%fused_computation.30 | convolution fusion | flops 706609152 | bytes 5177344 | tf_op jit(solution)/shard_map/dot_general | solution.py:32
  132.3 0.9 broadcast_in_dim.25
  133.2 5.1 %all-to-all-start.5 = ((f32[32,8,512]{2,1,0:T(8,128)}), f32[32,8,512]{2,1,0:T(8,128)}, u32[]{:S(2)}, u32[]{:S(2)}) async-start(f32[32,8,512]{2,1,0:T(8,128)} %broadcast_in_dim.25), calls=%async_computation.6 | async-start | bytes 1048576 | tf_op jit(solution)/shard_map/all_to_all | solution.py:43
  138.3 2.8 %fusion.11 = f32[512,384]{1,0:T(8,128)S(1)} fusion(bf16[1792,512]{1,0:T(8,128)(2,1)} %all-gather.3.cloned.1.call-done, bf16[2,1792,384]{2,1,0:T(8,128)(2,1)S(1)} %all_to_all.46), kind=kOutput, calls=%fused_computation.22 | convolution fusion | flops 704643072 | bytes 3997696 | tf_op jit(solution)/shard_map/dot_general | solution.py:32
  141.2 1.4 convolution_bitcast_fusion
  142.7 2.6 %convolution_add_fusion = f32[1792,384]{0,1:T(8,128)} fusion(f32[1792,384]{0,1:T(8,128)S(1)} %convolution_bitcast_fusion, bf16[1792,512]{1,0:T(8,128)(2,1)S(1)} %copy-done.4, f32[512,384]{1,0:T(8,128)S(1)} %fusion.11, f32[512,384]{1,0:T(8,128)S(1)} %copy-done.5), kind=kOutput, calls=%fused_computation.1 | convolution fusion | flops 707297280 | bytes 8912896 | tf_op jit(solution)/shard_map/dot_general | solution.py:32
  145.3 2.2 copy.32
  147.5 1.2 select_bitcast_fusion
  148.7 3.4 %collective-permute-start.5 = (f32[8,112,384]{2,1,0:T(8,128)}, f32[8,112,384]{2,1,0:T(8,128)}, u32[]{:S(2)}, u32[]{:S(2)}) collective-permute-start(f32[8,112,384]{2,1,0:T(8,128)} %select_bitcast_fusion), channel_id=1, source_target_pairs={{0,1},{1,0},{2,3},{3,2},{4,5},{5,4},{6,7},{7,6},{8,9},{9,8},{10,11... | collective-permute-start | bytes 4128776 | tf_op jit(solution)/shard_map/ppermute | solution.py:39
  152.1 1.5 all-to-all-done.5
  153.6 1.1 reduce_sum.27
  155.0 1.9 fusion.8
  156.9 1.9 fusion.1
  159.6 9.7 %all-to-all-start.6 = ((f32[16,8,640]{2,1,0:T(8,128)}), f32[16,8,640]{2,1,0:T(8,128)S(1)}, u32[]{:S(2)}, u32[]{:S(2)}) async-start(f32[16,8,640]{2,1,0:T(8,128)} %select_maximum_fusion), calls=%async_computation.7 | async-start | bytes 655360 | tf_op jit(solution)/shard_map/all_to_all | solution.py:43
  169.5 4.3 %fusion.10 = f32[512,1792]{1,0:T(8,128)} fusion(bf16[512,384]{1,0:T(8,128)(2,1)S(1)} %get-tuple-element.25, bf16[2,1792,384]{2,1,0:T(8,128)(2,1)} %copy-done), kind=kOutput, calls=%fused_computation.21 | convolution fusion | flops 704643072 | bytes 5439488 | tf_op jit(solution)/shard_map/dot_general | solution.py:32
  173.8 2.6 %fusion.6 = f32[8,112,384]{2,1,0:T(8,128)} fusion(f32[8,112,384]{2,1,0:T(8,128)} %collective-permute-done.5, f32[8,2,112,384]{3,2,1,0:T(8,128)S(1)} %bitcast.100, pred[]{:T(512)S(6)} %eq.6), kind=kLoop, calls=%fused_computation.12 | loop fusion | flops 688128 | bytes 5505025 | tf_op jit(solution)/shard_map/add | solution.py:183
  176.4 5.9 %all-to-all-done.6.parts = f32[16,8,640]{2,1,0:T(8,128)S(1)} async-done(((f32[16,8,640]{2,1,0:T(8,128)}), f32[16,8,640]{2,1,0:T(8,128)S(1)}, u32[]{:S(2)}, u32[]{:S(2)}) %all-to-all-start.6) | async-done | bytes 327712 | tf_op jit(solution)/shard_map/all_to_all | solution.py:43
  182.4 1.4 shard_map.94
  184.5 4.4 %all-to-all-start.7 = ((f32[32,8,128]{2,1,0:T(8,128)}), f32[32,8,128]{2,1,0:T(8,128)S(1)}, u32[]{:S(2)}, u32[]{:S(2)}) async-start(f32[32,8,128]{2,1,0:T(8,128)} %broadcast_in_dim.27), calls=%async_computation.8 | async-start | bytes 262144 | tf_op jit(solution)/shard_map/all_to_all | solution.py:43
  189.0 10.3 %all-to-all-done.7 = f32[32,8,128]{2,1,0:T(8,128)S(1)} async-done(((f32[32,8,128]{2,1,0:T(8,128)}), f32[32,8,128]{2,1,0:T(8,128)S(1)}, u32[]{:S(2)}, u32[]{:S(2)}) %all-to-all-start.7) | async-done | bytes 131104 | tf_op jit(solution)/shard_map/all_to_all | solution.py:43
  200.1 4.1 %all-to-all-start.8 = ((f32[16,8,128]{2,1,0:T(8,128)}), f32[16,8,128]{2,1,0:T(8,128)S(1)}, u32[]{:S(2)}, u32[]{:S(2)}) async-start(f32[16,8,128]{2,1,0:T(8,128)} %broadcast_in_dim.28), calls=%async_computation.9 | async-start | bytes 131072 | tf_op jit(solution)/shard_map/all_to_all | solution.py:43
  204.2 8.4 %all-to-all-done.8 = f32[16,8,128]{2,1,0:T(8,128)S(1)} async-done(((f32[16,8,128]{2,1,0:T(8,128)}), f32[16,8,128]{2,1,0:T(8,128)S(1)}, u32[]{:S(2)}, u32[]{:S(2)}) %all-to-all-start.8) | async-done | bytes 65568 | tf_op jit(solution)/shard_map/all_to_all | solution.py:43
  212.7 3.9 %fusion = bf16[1,512,1792]{2,1,0:T(8,128)(2,1)} fusion(bf16[48,512]{1,0:T(8,128)(2,1)S(1)} %constant_dynamic-update-slice_fusion.4, bf16[48,1792]{1,0:T(8,128)(2,1)S(1)} %constant_dynamic-update-slice_fusion.10, f32[512,1792]{1,0:T(8,128)} %fusion.10, bf16[1,512,1792]{2,1,0:T(8,128)(2,1)S(1)} %copy-done.1), kind=kOutput, calls=%fused_computation.3 | convolution fusion | flops 91750400 | bytes 7561216 | tf_op jit(solution)/shard_map/dot_general | solution.py:32
  216.6 1.6 convert_bitcast_fusion
  (82 shorter events, 15.8 us)
Async XLA Ops:
  18.5 14.1 %collective-permute-start = (bf16[224,384]{1,0:T(8,128)(2,1)S(1)}, bf16[224,384]{1,0:T(8,128)(2,1)S(1)}, u32[]{:S(2)}, u32[]{:S(2)}) collective-permute-start(bf16[224,384]{1,0:T(8,128)(2,1)S(1)} %bitcast.104), channel_id=1, source_target_pairs={{0,8},{2,10},{4,12},{6,14},{8,0},{10,2},{12,4},{14,6},{1,9},{3,11}... | collective-permute-start | bytes 516104 | tf_op jit(solution)/shard_map/ppermute | solution.py:39
  22.2 16.4 %all-to-all-start = ((bf16[4,2,56,512]{3,2,1,0:T(8,128)(2,1)}), bf16[4,2,56,512]{3,2,1,0:T(8,128)(2,1)S(1)}, u32[]{:S(2)}, u32[]{:S(2)}) async-start(bf16[4,2,56,512]{3,2,1,0:T(8,128)(2,1)} %broadcast_in_dim.20), calls=%async_computation | async-start | bytes 917504 | tf_op jit(solution)/shard_map/all_to_all | solution.py:43
  26.3 102.1 %all-gather.5.cloned.1.call-start = ((), (), s32[]{:S(2)}) async-start(), calls=%async_computation.11 | async-start | bytes 2064384 | tf_op jit(solution)/shard_map/all_gather | solution.py:133
  26.3 20.8 %collective-permute-start.2 = (bf16[224,384]{1,0:T(8,128)(2,1)S(1)}, bf16[224,384]{1,0:T(8,128)(2,1)S(1)}, u32[]{:S(2)}, u32[]{:S(2)}) collective-permute-start(bf16[224,384]{1,0:T(8,128)(2,1)S(1)} %bitcast.105), channel_id=1, source_target_pairs={{0,12},{2,14},{4,0},{6,2},{8,4},{10,6},{12,8},{14,10},{1,13},{3,15... | collective-permute-start | bytes 516104 | tf_op jit(solution)/shard_map/ppermute | solution.py:39
  28.2 21.6 %collective-permute-start.4 = (bf16[224,384]{1,0:T(8,128)(2,1)S(1)}, bf16[224,384]{1,0:T(8,128)(2,1)S(1)}, u32[]{:S(2)}, u32[]{:S(2)}) collective-permute-start(bf16[224,384]{1,0:T(8,128)(2,1)S(1)} %bitcast.106), channel_id=1, source_target_pairs={{0,4},{2,6},{4,8},{6,10},{8,12},{10,14},{12,0},{14,2},{1,5},{3,7},... | collective-permute-start | bytes 516104 | tf_op jit(solution)/shard_map/ppermute | solution.py:39
  32.6 13.8 %collective-permute-start.1 = (bf16[2,224,384]{2,1,0:T(8,128)(2,1)S(1)}, bf16[2,224,384]{2,1,0:T(8,128)(2,1)S(1)}, u32[]{:S(2)}, u32[]{:S(2)}) collective-permute-start(bf16[2,224,384]{2,1,0:T(8,128)(2,1)S(1)} %pad_maximum_fusion), channel_id=1, source_target_pairs={{0,14},{2,0},{4,2},{6,4},{8,6},{10,8},{12,10},{14,12},{1,15},{3,1}... | collective-permute-start | bytes 1032200 | tf_op jit(solution)/shard_map/ppermute | solution.py:39
  36.5 11.3 %collective-permute-start.3 = (bf16[2,224,384]{2,1,0:T(8,128)(2,1)S(1)}, bf16[2,224,384]{2,1,0:T(8,128)(2,1)S(1)}, u32[]{:S(2)}, u32[]{:S(2)}) collective-permute-start(bf16[2,224,384]{2,1,0:T(8,128)(2,1)S(1)} %pad_maximum_fusion), channel_id=1, source_target_pairs={{0,2},{2,4},{4,6},{6,8},{8,10},{10,12},{12,14},{14,0},{1,3},{3,5},... | collective-permute-start | bytes 1032200 | tf_op jit(solution)/shard_map/ppermute | solution.py:39
  58.5 8.1 %copy-start.9 = (bf16[56,512]{1,0:T(8,128)(2,1)S(1)}, bf16[56,512]{1,0:T(8,128)(2,1)}, u32[]{:S(2)}) copy-start(bf16[56,512]{1,0:T(8,128)(2,1)} %param.9) | copy-start | bytes 172036
  66.5 71.8 %copy-start = (bf16[2,1792,384]{2,1,0:T(8,128)(2,1)}, bf16[2,1792,384]{2,1,0:T(8,128)(2,1)S(1)}, u32[]{:S(2)}) copy-start(bf16[2,1792,384]{2,1,0:T(8,128)(2,1)S(1)} %all_to_all.46) | copy-start | bytes 8257540
  67.4 27.4 %all-to-all-start.3 = ((bf16[8,56,512]{2,1,0:T(8,128)(2,1)}), bf16[8,56,512]{2,1,0:T(8,128)(2,1)S(1)}, u32[]{:S(2)}, u32[]{:S(2)}) async-start(bf16[8,56,512]{2,1,0:T(8,128)(2,1)} %broadcast_in_dim.23), calls=%async_computation.3 | async-start | bytes 917504 | tf_op jit(solution)/shard_map/all_to_all | solution.py:43
  77.4 60.9 %all-gather.3.cloned.1.call-start = ((), (), s32[]{:S(2)}) async-start(), calls=%async_computation.10 | async-start | bytes 2064384 | tf_op jit(solution)/shard_map/all_gather | solution.py:134
  78.2 22.4 %copy-start.8 = (f32[8,1792]{1,0:T(8,128)S(1)}, f32[8,1792]{1,0:T(8,128)}, u32[]{:S(2)}) copy-start(f32[8,1792]{1,0:T(8,128)} %param.13) | copy-start | bytes 172036
  96.1 27.2 %all-to-all-start.4 = ((bf16[4,8,56,512]{3,2,1,0:T(8,128)(2,1)}), bf16[4,8,56,512]{3,2,1,0:T(8,128)(2,1)}, u32[]{:S(2)}, u32[]{:S(2)}) async-start(bf16[4,8,56,512]{3,2,1,0:T(8,128)(2,1)} %broadcast_in_dim.24), calls=%async_computation.4 | async-start | bytes 3670016 | tf_op jit(solution)/shard_map/all_to_all | solution.py:43
  125.1 1.2 copy-start.2
  133.2 20.4 %all-to-all-start.5 = ((f32[32,8,512]{2,1,0:T(8,128)}), f32[32,8,512]{2,1,0:T(8,128)}, u32[]{:S(2)}, u32[]{:S(2)}) async-start(f32[32,8,512]{2,1,0:T(8,128)} %broadcast_in_dim.25), calls=%async_computation.6 | async-start | bytes 1048576 | tf_op jit(solution)/shard_map/all_to_all | solution.py:43
  138.3 2.8 %copy-start.3 = (bf16[4,8,56,512]{3,2,0,1:T(8,128)(2,1)S(1)}, bf16[4,8,56,512]{3,2,0,1:T(8,128)(2,1)}, u32[]{:S(2)}) copy-start(bf16[4,8,56,512]{3,2,0,1:T(8,128)(2,1)} %copy-done.2) | copy-start | bytes 5505028
  138.3 2.8 %copy-start.5 = (f32[512,384]{1,0:T(8,128)S(1)}, f32[512,384]{1,0:T(8,128)}, u32[]{:S(2)}) copy-start(f32[512,384]{1,0:T(8,128)} %convolution_bitcast_fusion.1) | copy-start | bytes 2359300
  138.3 2.8 %copy-start.7 = (f32[512,384]{1,0:T(8,128)S(1)}, f32[512,384]{1,0:T(8,128)}, u32[]{:S(2)}) copy-start(f32[512,384]{1,0:T(8,128)} %get-tuple-element.26) | copy-start | bytes 2359300
  141.2 1.5 copy-start.4
  148.7 25.1 %collective-permute-start.5 = (f32[8,112,384]{2,1,0:T(8,128)}, f32[8,112,384]{2,1,0:T(8,128)}, u32[]{:S(2)}, u32[]{:S(2)}) collective-permute-start(f32[8,112,384]{2,1,0:T(8,128)} %select_bitcast_fusion), channel_id=1, source_target_pairs={{0,1},{1,0},{2,3},{3,2},{4,5},{5,4},{6,7},{7,6},{8,9},{9,8},{10,11... | collective-permute-start | bytes 4128776 | tf_op jit(solution)/shard_map/ppermute | solution.py:39
  159.6 22.8 %all-to-all-start.6 = ((f32[16,8,640]{2,1,0:T(8,128)}), f32[16,8,640]{2,1,0:T(8,128)S(1)}, u32[]{:S(2)}, u32[]{:S(2)}) async-start(f32[16,8,640]{2,1,0:T(8,128)} %select_maximum_fusion), calls=%async_computation.7 | async-start | bytes 655360 | tf_op jit(solution)/shard_map/all_to_all | solution.py:43
  169.3 47.3 %reduce-scatter.2.cloned.1.call-start = ((), (), s32[]{:S(2)}) async-start(), calls=%async_computation.12 | async-start | bytes 1548288 | tf_op jit(solution)/shard_map/reduce_scatter | solution.py:184
  176.4 36.3 %copy-start.1 = (bf16[1,512,1792]{2,1,0:T(8,128)(2,1)S(1)}, bf16[1,512,1792]{2,1,0:T(8,128)(2,1)}, u32[]{:S(2)}) copy-start(bf16[1,512,1792]{2,1,0:T(8,128)(2,1)} %param.12) | copy-start | bytes 5505028
  184.5 14.8 %all-to-all-start.7 = ((f32[32,8,128]{2,1,0:T(8,128)}), f32[32,8,128]{2,1,0:T(8,128)S(1)}, u32[]{:S(2)}, u32[]{:S(2)}) async-start(f32[32,8,128]{2,1,0:T(8,128)} %broadcast_in_dim.27), calls=%async_computation.8 | async-start | bytes 262144 | tf_op jit(solution)/shard_map/all_to_all | solution.py:43
  200.1 12.5 %all-to-all-start.8 = ((f32[16,8,128]{2,1,0:T(8,128)}), f32[16,8,128]{2,1,0:T(8,128)S(1)}, u32[]{:S(2)}, u32[]{:S(2)}) async-start(f32[16,8,128]{2,1,0:T(8,128)} %broadcast_in_dim.28), calls=%async_computation.9 | async-start | bytes 131072 | tf_op jit(solution)/shard_map/all_to_all | solution.py:43
  212.6 4.0 %copy-start.6 = (f32[8,1792]{1,0:T(8,128)}, f32[8,1792]{1,0:T(8,128)S(1)}, u32[]{:S(2)}) copy-start(f32[8,1792]{1,0:T(8,128)S(1)} %get-tuple-element.8) | copy-start | bytes 172036
Sparse Core Ops, SparseCore 0:
  39.6 46.6 all-gather.4
  88.3 45.8 all-gather.2
  176.6 34.6 reduce-scatter.1

commit v2 on v1

--- a/solution.py
+++ b/solution.py
@@ -63,6 +63,33 @@
 def fold3(value):
     n = value.shape[0] // 3
     return value[:n] + (value[n : 2 * n] + value[2 * n :])
+
+
+def place_kernel(count, plan, at, *refs):
+    blocks, out = refs[:-1], refs[-1]
+    rows = out.shape[1]
+    for index, part, offset in plan:
+        slot = lax.rem(at[0] + offset, count)
+        if part == "top":
+            out[slot, : rows // 2, :] = blocks[index][...]
+        elif part == "end":
+            out[slot, rows // 2 :, :] = blocks[index][...]
+        elif part is None:
+            out[slot] = blocks[index][...]
+        else:
+            out[slot] = blocks[index][part]
+
+
+def place(blocks, plan, count, at):
+    return pl.pallas_call(
+        lambda *refs: place_kernel(count, plan, *refs),
+        out_shape=jax.ShapeDtypeStruct((count,) + blocks[0].shape, blocks[0].dtype),
+        in_specs=[pl.BlockSpec(memory_space=pltpu.SMEM)]
+        + [pl.BlockSpec(memory_space=pltpu.VMEM)] * len(blocks),
+        out_specs=pl.BlockSpec(memory_space=pltpu.VMEM),
+        compiler_params=pltpu.CompilerParams(vmem_limit_bytes=24 * 1024 * 1024),
+        name="place",
+    )(at.astype(jnp.int32).reshape(1), *blocks)
 
 
 def orth_kernel(mine, parts, orth, transform, rows):
@@ -110,41 +137,81 @@
     )(mine, parts)
 
 
+def grad_share(d_hidden, up_val, slope, active, weights):
+    d_gate = (d_hidden * up_val * slope).astype(bf16)
+    d_up = (d_hidden * active).astype(bf16)
+    grads = contract(weights, jnp.concatenate([d_gate, d_up]), 1, 0)
+    return grads
+
+
+def pass_kernel(value, _, out):
+    out[...] = value[...]
+
+
+def when_ready(value, other):
+    return pl.pallas_call(
+        pass_kernel,
+        out_shape=jax.ShapeDtypeStruct(value.shape, value.dtype),
+        in_specs=[pl.BlockSpec(memory_space=pltpu.VMEM), pl.BlockSpec(memory_space=pl.ANY)],
+        out_specs=pl.BlockSpec(memory_space=pltpu.VMEM),
+        name="when_ready",
+    )(value, other)
+
+
 def per_device(tokens, cotangent, gate_weight, up_weight, down_weight, error_buffer, q_init):
+    x_at = lax.axis_index("x")
     y_at = lax.axis_index("y")
     c_at = lax.axis_index("c")
     errors = error_buffer[0]
     units = gate_weight.shape[1]
 
-    pair = swap(jnp.stack([tokens.T, cotangent.T]), ("c",))
-    block = pair.reshape(-1, pair.shape[-1])
+    first = c_at == 0
+
+    both_weights = jnp.concatenate([gate_weight, up_weight], axis=1)
+    weights_x = gather(both_weights, ("x",)).reshape(-1, 2 * units)
+    weights_x, block, down = lax.optimization_barrier(
+        (weights_x, jnp.stack([tokens.T, cotangent.T]), down_weight.T)
+    )
+    weights = lax.all_gather(weights_x, "z", axis=0, tiled=True)
+
+    down_z = gather(down, ("z",)).reshape(-1, units)
     far = shift(block, "y", 4)
     back2 = shift(block, "y", 2)
     fore2 = shift(block, "y", -2)
+    down_z, block, far = lax.optimization_barrier((down_z, block, far))
+    down_all = gather(down_z, ("x",))
     both = jnp.stack([block, far])
     back = shift(both, "y", 1)
     fore = shift(both, "y", -1)
-    in_turn = jnp.stack([block, fore[0], fore2, back[1], far, fore[1], back2, back[0]])
-    twice = jnp.concatenate([in_turn, in_turn], axis=0)
-    ordered = lax.dynamic_slice_in_dim(twice, (Y - y_at) % Y, Y, axis=0)
-    inputs, upstream = gather(ordered.reshape(-1, block.shape[-1]), ("c",))
-
-    side = gather(jnp.stack([up_weight, down_weight.T]), ("x",))
-    up_all = lax.all_gather(side[:, 0].reshape(-1, units), "z", axis=0, tiled=True)
-    down_all = lax.all_gather(side[:, 1].reshape(-1, units), "z", axis=0, tiled=True)
-    gate_z = gather(gate_weight, ("z",))
-    gate_all = gather(gate_z, ("x",)).transpose(1, 0, 2, 3).reshape(-1, units)
-
-    gate = contract(gate_all, inputs, 0, 0)
-    up_val = contract(up_all, inputs, 0, 0)
+    mine = place(
+        [block, far, back2, fore2, back, fore],
+        [(0, None, 0), (1, None, 4), (2, None, 6), (3, None, 2), (4, 0, 7), (4, 1, 3), (5, 0, 1), (5, 1, 5)],
+        Y,
+        y_at,
+    )
+    mine, down_all = lax.optimization_barrier((mine, down_all))
+    other = shift(mine, "c", 1)
+    even = jnp.where(first, mine, other)
+    odd = jnp.where(first, other, mine)
+    inputs, upstream = (
+        jnp.stack([even[:, kind], odd[:, kind]], axis=1).reshape(-1, block.shape[-1])
+        for kind in (0, 1)
+    )
+    gate_up = contract(weights, inputs, 0, 0)
+    gate, up_val = gate_up[:units], gate_up[units:]
     active, slope = gelu_parts(gate)
     hidden = (active * up_val).astype(bf16)
+    hidden, down_all = lax.optimization_barrier((hidden, down_all))
+    down_all = down_all.reshape(X, Z, -1, units).transpose(1, 0, 2, 3).reshape(-1, units)
+    d_hidden = contract(down_all, upstream, 0, 0)
 
     q_stack = stack3(q_init)
     cot_q = stack3(fold3(contract(q_stack, upstream, 1, 0)))
     err_q = fold3(contract(q_stack, errors, 1, 1))
     p_part = fold3(contract(cot_q, hidden, 1, 1)) + err_q
-    p_sum = jnp.sum(gather(p_part, ("z", "x")), axis=0)
+    p_all = gather(p_part, ("z", "x"))
+    grads = grad_share(d_hidden, up_val, slope, active, weights)
+    p_sum = when_ready(jnp.sum(p_all, axis=0), grads)
 
     p_stack = stack3(p_sum)
     hid_p = stack3(fold3(contract(p_stack, hidden, 1, 0)))
@@ -173,15 +240,7 @@
     local_grad = contract(hidden, upstream, 1, 1)
     new_error = (local_grad + errors.astype(f32) - approx).astype(bf16)[None]
 
-    d_hidden = contract(down_all, upstream, 0, 0)
-    d_gate = (d_hidden * up_val * slope).astype(bf16)
-    d_up = (d_hidden * active).astype(bf16)
-    grads = contract(gate_all, d_gate, 1, 0) + contract(up_all, d_up, 1, 0)
-    grads = grads.reshape(Y, C, -1, grads.shape[-1])
-    keep = jnp.where(c_at == 0, grads[:, 0], grads[:, 1])
-    give = jnp.where(c_at == 0, grads[:, 1], grads[:, 0])
-    chip = keep + shift(give, "c", 1)
-    grad_tokens = lax.psum_scatter(chip, "y", scatter_dimension=0, tiled=False)
+    grad_tokens = lax.psum_scatter(grads, ("y", "c"), scatter_dimension=0, tiled=True)
     return (grad_tokens.astype(bf16).T, new_error, q_avg)
 
 

time: 226 us -> 187 us (0.83)
  blocking collectives: 18.4 us -> 0 us
  local copies, waits for them, and re-layouts: 24 us -> 9.21 us
  starting transfers between devices: 59 us -> 73.4 us
  waiting for transfers between devices: 70.8 us -> 56.8 us
  matrix products: 27.4 us -> 22.5 us
  other arithmetic: 9.41 us -> 6.83 us
    all_to_all x2 -> x0, blocking collectives: 18.4 us -> none  [swap(): return lax.all_to_all(stacked, axes, 0, 0, tiled=True)]
    all_to_all x7, waiting for transfers between devices: 63 us -> 46 us  [swap(): return lax.all_to_all(stacked, axes, 0, 0, tiled=True)]
    ppermute x6, starting transfers between devices: 16.9 us -> 31.1 us  [shift(): return lax.ppermute(value, axis, [(i, (i + step) % n) for i in range(n)])]
    unnamed x35 -> x20, local copies, waits for them, and re-layouts: 11.6 us -> 2.07 us
    dot_general x13 -> x11, matrix products: 27.3 us -> 22.3 us  [contract(): lax.dot_general(left, right, (((dim_left,), (dim_right,)), ((), ())), pre...]
    ppermute x6, waiting for transfers between devices: 7.07 us -> 10.8 us  [shift(): return lax.ppermute(value, axis, [(i, (i + step) % n) for i in range(n)])]
    add x1 -> x0, other arithmetic: 2.63 us -> none  [per_device(): chip = keep + shift(give, 'c', 1)]
    broadcast_in_dim x7 -> x6, local copies, waits for them, and re-layouts: 5.44 us -> 5.16 us  [gather(): return swap(jnp.broadcast_to(value[None], (n,) + value.shape), axes)]
  transfers between devices with their start and end apart: 16 -> 15, of which waited for: 8 -> 10; matrix products, arithmetic and copies ran while one was open for 25% -> 15% of each run, Pallas kernels for 1% -> 2%
where the time goes in v2:
time: 187 us; the launch traced here: 186 us
  starting transfers between devices  73.4 us (39%)
  waiting for transfers between devices  56.8 us (30%)
  matrix products  22.5 us (12%)
  between operations  14.5 us (8%)
  local copies, waits for them, and re-layouts  9.21 us (5%)
  other arithmetic  6.83 us (4%)
  Pallas kernels  2.99 us (2%)
    all_to_all x7, waiting for transfers between devices, swap(): return lax.all_to_all(stacked, axes, 0, 0, tiled=True)  46 us
    all_to_all x7, starting transfers between devices, swap(): return lax.all_to_all(stacked, axes, 0, 0, tiled=True)  42.3 us
    ppermute x6, starting transfers between devices, shift(): return lax.ppermute(value, axis, [(i, (i + step) % n) for i in range(n)])  31.1 us
    dot_general x11, matrix products, contract(): lax.dot_general(left, right, (((dim_left,), (dim_right,)), ((), ())), pre...  22.3 us
    ppermute x6, waiting for transfers between devices, shift(): return lax.ppermute(value, axis, [(i, (i + step) % n) for i in range(n)])  10.8 us
    broadcast_in_dim x6, local copies, waits for them, and re-layouts, gather(): return swap(jnp.broadcast_to(value[None], (n,) + value.shape), axes)  5.16 us
  transfers between devices with their start and end apart: 15, of which 10 were waited for; matrix products, arithmetic and copies ran while one was open for 15% of the time, Pallas kernels for 2%

profile of v2, /device:TPU:1, one launch (start us, length us, event | category | flops | bytes accessed | tf_op | source)
XLA Modules:
  0.0 186.2 jit_solution(9873426322571302800)
XLA Ops:
  7.2 0.9 pad_maximum_fusion.4
  8.1 0.8 broadcast_in_dim.16
  8.9 4.8 %all-to-all-start = ((bf16[4,56,1024]{2,1,0:T(8,128)(2,1)}), bf16[4,56,1024]{2,1,0:T(8,128)(2,1)S(1)}, u32[]{:S(2)}, u32[]{:S(2)}) async-start(bf16[4,56,1024]{2,1,0:T(8,128)(2,1)} %broadcast_in_dim.16), calls=%async_computation | async-start | bytes 917504 | tf_op jit(solution)/shard_map/all_to_all | solution.py:43
  13.8 6.5 %all-to-all-done = bf16[4,56,1024]{2,1,0:T(8,128)(2,1)S(1)} async-done(((bf16[4,56,1024]{2,1,0:T(8,128)(2,1)}), bf16[4,56,1024]{2,1,0:T(8,128)(2,1)S(1)}, u32[]{:S(2)}, u32[]{:S(2)}) %all-to-all-start) | async-done | bytes 458784 | tf_op jit(solution)/shard_map/all_to_all | solution.py:43
  20.3 0.8 copy-done.3
  21.2 0.8 broadcast_in_dim.17
  22.0 11.0 %all-to-all-start.1 = ((bf16[8,56,512]{2,1,0:T(8,128)(2,1)}), bf16[8,56,512]{2,1,0:T(8,128)(2,1)S(1)}, u32[]{:S(2)}, u32[]{:S(2)}) async-start(bf16[8,56,512]{2,1,0:T(8,128)(2,1)} %broadcast_in_dim.17), calls=%async_computation.1 | async-start | bytes 917504 | tf_op jit(solution)/shard_map/all_to_all | solution.py:43
  33.0 7.4 %collective-permute-start = (bf16[2,112,384]{2,1,0:T(8,128)(2,1)S(1)}, bf16[2,112,384]{2,1,0:T(8,128)(2,1)S(1)}, u32[]{:S(2)}, u32[]{:S(2)}) collective-permute-start(bf16[2,112,384]{2,1,0:T(8,128)(2,1)S(1)} %pad_maximum_fusion.3.refs_1_), channel_id=1, source_target_pairs={{0,8},{2,10},{4,12},{6,14},{8,0},{10,2},{12,4},{14,6},{1,9},{3,11}... | collective-permute-start | bytes 516104 | tf_op jit(solution)/shard_map/ppermute | solution.py:39
  40.4 2.9 %collective-permute-done.refs_2_ = bf16[2,112,384]{2,1,0:T(8,128)(2,1)S(1)} collective-permute-done((bf16[2,112,384]{2,1,0:T(8,128)(2,1)S(1)}, bf16[2,112,384]{2,1,0:T(8,128)(2,1)S(1)}, u32[]{:S(2)}, u32[]{:S(2)}) %collective-permute-start) | collective-permute-done | bytes 172064 | tf_op jit(solution)/shard_map/ppermute | solution.py:39
  43.3 3.3 %all-to-all-done.1 = bf16[8,56,512]{2,1,0:T(8,128)(2,1)S(1)} async-done(((bf16[8,56,512]{2,1,0:T(8,128)(2,1)}), bf16[8,56,512]{2,1,0:T(8,128)(2,1)S(1)}, u32[]{:S(2)}, u32[]{:S(2)}) %all-to-all-start.1) | async-done | bytes 458784 | tf_op jit(solution)/shard_map/all_to_all | solution.py:43
  46.6 1.4 broadcast_in_dim.18
  48.0 4.4 %all-to-all-start.2 = ((bf16[4,448,512]{2,1,0:T(8,128)(2,1)}), bf16[4,448,512]{2,1,0:T(8,128)(2,1)}, u32[]{:S(2)}, u32[]{:S(2)}) async-start(bf16[4,448,512]{2,1,0:T(8,128)(2,1)} %broadcast_in_dim.18), calls=%async_computation.2 | async-start | bytes 3670016 | tf_op jit(solution)/shard_map/all_to_all | solution.py:43
  52.4 3.2 %collective-permute-start.3 = (bf16[2,2,112,384]{3,2,1,0:T(8,128)(2,1)S(1)}, bf16[2,2,112,384]{3,2,1,0:T(8,128)(2,1)S(1)}, u32[]{:S(2)}, u32[]{:S(2)}) collective-permute-start(bf16[2,2,112,384]{3,2,1,0:T(8,128)(2,1)S(1)} %pad_maximum_fusion.2), channel_id=1, source_target_pairs={{0,2},{2,4},{4,6},{6,8},{8,10},{10,12},{12,14},{14,0},{1,3},{3,5},... | collective-permute-start | bytes 1032200 | tf_op jit(solution)/shard_map/ppermute | solution.py:39
  55.7 4.9 %collective-permute-start.4 = (bf16[2,2,112,384]{3,2,1,0:T(8,128)(2,1)S(1)}, bf16[2,2,112,384]{3,2,1,0:T(8,128)(2,1)S(1)}, u32[]{:S(2)}, u32[]{:S(2)}) collective-permute-start(bf16[2,2,112,384]{3,2,1,0:T(8,128)(2,1)S(1)} %pad_maximum_fusion.2), channel_id=1, source_target_pairs={{0,14},{2,0},{4,2},{6,4},{8,6},{10,8},{12,10},{14,12},{1,15},{3,1}... | collective-permute-start | bytes 1032200 | tf_op jit(solution)/shard_map/ppermute | solution.py:39
  60.6 2.5 %collective-permute-start.1 = (bf16[2,112,384]{2,1,0:T(8,128)(2,1)S(1)}, bf16[2,112,384]{2,1,0:T(8,128)(2,1)S(1)}, u32[]{:S(2)}, u32[]{:S(2)}) collective-permute-start(bf16[2,112,384]{2,1,0:T(8,128)(2,1)S(1)} %pad_maximum_fusion.3.refs_1_), channel_id=1, source_target_pairs={{0,4},{2,6},{4,8},{6,10},{8,12},{10,14},{12,0},{14,2},{1,5},{3,7},... | collective-permute-start | bytes 516104 | tf_op jit(solution)/shard_map/ppermute | solution.py:39
  63.1 4.9 %collective-permute-start.2 = (bf16[2,112,384]{2,1,0:T(8,128)(2,1)S(1)}, bf16[2,112,384]{2,1,0:T(8,128)(2,1)S(1)}, u32[]{:S(2)}, u32[]{:S(2)}) collective-permute-start(bf16[2,112,384]{2,1,0:T(8,128)(2,1)S(1)} %pad_maximum_fusion.3.refs_1_), channel_id=1, source_target_pairs={{0,12},{2,14},{4,0},{6,2},{8,4},{10,6},{12,8},{14,10},{1,13},{3,15... | collective-permute-start | bytes 516104 | tf_op jit(solution)/shard_map/ppermute | solution.py:39
  68.0 4.9 %collective-permute-done.1.refs_3_ = bf16[2,112,384]{2,1,0:T(8,128)(2,1)S(1)} collective-permute-done((bf16[2,112,384]{2,1,0:T(8,128)(2,1)S(1)}, bf16[2,112,384]{2,1,0:T(8,128)(2,1)S(1)}, u32[]{:S(2)}, u32[]{:S(2)}) %collective-permute-start.1) | collective-permute-done | bytes 172064 | tf_op jit(solution)/shard_map/ppermute | solution.py:39
  72.9 2.4 %collective-permute-done.2.refs_4_ = bf16[2,112,384]{2,1,0:T(8,128)(2,1)S(1)} collective-permute-done((bf16[2,112,384]{2,1,0:T(8,128)(2,1)S(1)}, bf16[2,112,384]{2,1,0:T(8,128)(2,1)S(1)}, u32[]{:S(2)}, u32[]{:S(2)}) %collective-permute-start.2) | collective-permute-done | bytes 172064 | tf_op jit(solution)/shard_map/ppermute | solution.py:39
  75.4 8.1 %collective-permute-start.5 = (bf16[8,2,112,384]{3,2,1,0:T(8,128)(2,1)S(1)}, bf16[8,2,112,384]{3,2,1,0:T(8,128)(2,1)S(1)}, u32[]{:S(2)}, u32[]{:S(2)}) collective-permute-start(bf16[8,2,112,384]{3,2,1,0:T(8,128)(2,1)S(1)} %place.1), channel_id=1, source_target_pairs={{0,1},{1,0},{2,3},{3,2},{4,5},{5,4},{6,7},{7,6},{8,9},{9,8},{10,11... | collective-permute-start | bytes 4128776 | tf_op jit(solution)/shard_map/ppermute | solution.py:39
  83.6 2.1 %fusion.3 = f32[24,512]{1,0:T(8,128)S(1)} fusion(bf16[1,512,1792]{2,1,0:T(8,128)(2,1)} %param.12, bf16[8,1792]{1,0:T(8,128)(2,1)S(1)} %get-tuple-element.42, bf16[8,1792]{1,0:T(8,128)(2,1)S(1)} %get-tuple-element.43, bf16[8,1792]{1,0:T(8,128)(2,1)S(1)} %get-tuple-element.41), kind=kOutput, calls=%fused_computation.4 | convolution fusion | flops 44298240 | bytes 1970176 | tf_op jit(solution)/shard_map/dot_general | solution.py:32
  85.7 0.6 collective-permute-done.5
  86.9 1.2 pad_maximum_fusion
  88.6 4.5 %fusion.58 = f32[1024,384]{1,0:T(8,128)S(1)} fusion(bf16[1792,1024]{1,0:T(8,128)(2,1)} %all-gather.2.cloned.1.call-done, bf16[1792,384]{1,0:T(8,128)(2,1)} %bitcast.61), kind=kOutput, calls=%fused_computation.118 | convolution fusion | flops 1409286144 | bytes 6619136 | tf_op jit(solution)/shard_map/dot_general | solution.py:32
  93.5 0.8 copy-done.1
  94.5 0.9 broadcast_in_dim.19
  95.3 5.9 %all-to-all-start.3 = ((f32[32,8,512]{2,1,0:T(8,128)}), f32[32,8,512]{2,1,0:T(8,128)S(1)}, u32[]{:S(2)}, u32[]{:S(2)}) async-start(f32[32,8,512]{2,1,0:T(8,128)} %broadcast_in_dim.19), calls=%async_computation.4 | async-start | bytes 1048576 | tf_op jit(solution)/shard_map/all_to_all | solution.py:43
  101.3 1.7 copy.11
  103.0 1.5 fusion.11
  105.0 3.7 %fusion.12._ = f32[1792,384]{1,0:T(8,128)} fusion(bf16[1792,1024]{1,0:T(8,128)(2,1)S(1)} %copy-done.9, bf16[512,384]{1,0:T(8,128)(2,1)S(1)} %get-tuple-element.36, bf16[512,384]{1,0:T(8,128)(2,1)S(1)} %get-tuple-element.35), kind=kOutput, calls=%fused_computation.20 | convolution fusion | flops 1410859008 | bytes 7208960 | tf_op jit(solution)/shard_map/dot_general | solution.py:32
  108.8 9.1 %all-to-all-done.3 = f32[32,8,512]{2,1,0:T(8,128)S(1)} async-done(((f32[32,8,512]{2,1,0:T(8,128)}), f32[32,8,512]{2,1,0:T(8,128)S(1)}, u32[]{:S(2)}, u32[]{:S(2)}) %all-to-all-start.3) | async-done | bytes 524320 | tf_op jit(solution)/shard_map/all_to_all | solution.py:43
  117.8 0.6 reduce_sum.27.value
  118.5 1.5 when_ready.1
  120.0 0.7 reduce-precision_convert_fusion.7
  120.7 1.2 fusion.45
  122.3 0.6 fusion.30
  122.9 0.7 select_maximum_fusion
  123.7 7.2 %all-to-all-start.4 = ((f32[16,8,640]{2,1,0:T(8,128)}), f32[16,8,640]{2,1,0:T(8,128)S(1)}, u32[]{:S(2)}, u32[]{:S(2)}) async-start(f32[16,8,640]{2,1,0:T(8,128)} %select_maximum_fusion), calls=%async_computation.5 | async-start | bytes 655360 | tf_op jit(solution)/shard_map/all_to_all | solution.py:43
  130.9 3.9 %fusion.59 = f32[512,1792]{1,0:T(8,128)} fusion(bf16[512,384]{1,0:T(8,128)(2,1)} %copy-done.1, bf16[1792,384]{1,0:T(8,128)(2,1)S(1)} %bitcast.57), kind=kOutput, calls=%fused_computation.119 | convolution fusion | flops 704643072 | bytes 5439488 | tf_op jit(solution)/shard_map/dot_general | solution.py:32
  134.8 10.6 %all-to-all-done.4.parts = f32[16,8,640]{2,1,0:T(8,128)S(1)} async-done(((f32[16,8,640]{2,1,0:T(8,128)}), f32[16,8,640]{2,1,0:T(8,128)S(1)}, u32[]{:S(2)}, u32[]{:S(2)}) %all-to-all-start.4) | async-done | bytes 327712 | tf_op jit(solution)/shard_map/all_to_all | solution.py:43
  145.4 0.7 broadcast_in_dim.21
  146.1 4.2 %all-to-all-start.5 = ((f32[32,8,128]{2,1,0:T(8,128)}), f32[32,8,128]{2,1,0:T(8,128)S(1)}, u32[]{:S(2)}, u32[]{:S(2)}) async-start(f32[32,8,128]{2,1,0:T(8,128)} %broadcast_in_dim.21), calls=%async_computation.6 | async-start | bytes 262144 | tf_op jit(solution)/shard_map/all_to_all | solution.py:43
  150.2 1.4 shard_map.94
  151.7 8.5 %all-to-all-done.5 = f32[32,8,128]{2,1,0:T(8,128)S(1)} async-done(((f32[32,8,128]{2,1,0:T(8,128)}), f32[32,8,128]{2,1,0:T(8,128)S(1)}, u32[]{:S(2)}, u32[]{:S(2)}) %all-to-all-start.5) | async-done | bytes 131104 | tf_op jit(solution)/shard_map/all_to_all | solution.py:43
  160.3 0.6 broadcast_in_dim.22
  161.0 4.7 %all-to-all-start.6 = ((f32[16,8,128]{2,1,0:T(8,128)}), f32[16,8,128]{2,1,0:T(8,128)S(1)}, u32[]{:S(2)}, u32[]{:S(2)}) async-start(f32[16,8,128]{2,1,0:T(8,128)} %broadcast_in_dim.22), calls=%async_computation.7 | async-start | bytes 131072 | tf_op jit(solution)/shard_map/all_to_all | solution.py:43
  165.7 8.0 %all-to-all-done.6 = f32[16,8,128]{2,1,0:T(8,128)S(1)} async-done(((f32[16,8,128]{2,1,0:T(8,128)}), f32[16,8,128]{2,1,0:T(8,128)S(1)}, u32[]{:S(2)}, u32[]{:S(2)}) %all-to-all-start.6) | async-done | bytes 65568 | tf_op jit(solution)/shard_map/all_to_all | solution.py:43
  173.8 3.9 %fusion = bf16[1,512,1792]{2,1,0:T(8,128)(2,1)} fusion(bf16[48,512]{1,0:T(8,128)(2,1)S(1)} %constant_dynamic-update-slice_fusion, bf16[48,1792]{1,0:T(8,128)(2,1)S(1)} %constant_dynamic-update-slice_fusion.6, f32[512,1792]{1,0:T(8,128)} %fusion.59, bf16[1,512,1792]{2,1,0:T(8,128)(2,1)S(1)} %copy-done), kind=kOutput, calls=%fused_computation.1 | convolution fusion | flops 91750400 | bytes 7561216 | tf_op jit(solution)/shard_map/dot_general | solution.py:32
  177.8 1.6 convert_bitcast_fusion
  (60 shorter events, 3.1 us)
Async XLA Ops:
  7.2 6.6 %copy-start.5 = (bf16[384,112]{0,1:T(8,128)(2,1)S(1)}, bf16[384,112]{0,1:T(8,128)(2,1)}, u32[]{:S(2)}) copy-start(bf16[384,112]{0,1:T(8,128)(2,1)} %param.8) | copy-start | bytes 258052
  7.2 6.6 %copy-start.6 = (bf16[384,112]{0,1:T(8,128)(2,1)S(1)}, bf16[384,112]{0,1:T(8,128)(2,1)}, u32[]{:S(2)}) copy-start(bf16[384,112]{0,1:T(8,128)(2,1)} %param.7) | copy-start | bytes 258052
  7.2 14.0 %copy-start.8 = (bf16[512,56]{0,1:T(8,128)(2,1)S(1)}, bf16[512,56]{0,1:T(8,128)(2,1)}, u32[]{:S(2)}) copy-start(bf16[512,56]{0,1:T(8,128)(2,1)} %param.11) | copy-start | bytes 172036
  8.9 11.4 %all-to-all-start = ((bf16[4,56,1024]{2,1,0:T(8,128)(2,1)}), bf16[4,56,1024]{2,1,0:T(8,128)(2,1)S(1)}, u32[]{:S(2)}, u32[]{:S(2)}) async-start(bf16[4,56,1024]{2,1,0:T(8,128)(2,1)} %broadcast_in_dim.16), calls=%async_computation | async-start | bytes 917504 | tf_op jit(solution)/shard_map/all_to_all | solution.py:43
  13.8 74.9 %all-gather.2.cloned.1.call-start = ((), (), s32[]{:S(2)}) async-start(), calls=%async_computation.8 | async-start | bytes 4128768 | tf_op jit(solution)/shard_map/all_gather | solution.py:175
  20.3 0.8 copy-start.3
  22.0 24.6 %all-to-all-start.1 = ((bf16[8,56,512]{2,1,0:T(8,128)(2,1)}), bf16[8,56,512]{2,1,0:T(8,128)(2,1)S(1)}, u32[]{:S(2)}, u32[]{:S(2)}) async-start(bf16[8,56,512]{2,1,0:T(8,128)(2,1)} %broadcast_in_dim.17), calls=%async_computation.1 | async-start | bytes 917504 | tf_op jit(solution)/shard_map/all_to_all | solution.py:43
  33.0 10.3 %collective-permute-start = (bf16[2,112,384]{2,1,0:T(8,128)(2,1)S(1)}, bf16[2,112,384]{2,1,0:T(8,128)(2,1)S(1)}, u32[]{:S(2)}, u32[]{:S(2)}) collective-permute-start(bf16[2,112,384]{2,1,0:T(8,128)(2,1)S(1)} %pad_maximum_fusion.3.refs_1_), channel_id=1, source_target_pairs={{0,8},{2,10},{4,12},{6,14},{8,0},{10,2},{12,4},{14,6},{1,9},{3,11}... | collective-permute-start | bytes 516104 | tf_op jit(solution)/shard_map/ppermute | solution.py:39
  48.0 27.5 %all-to-all-start.2 = ((bf16[4,448,512]{2,1,0:T(8,128)(2,1)}), bf16[4,448,512]{2,1,0:T(8,128)(2,1)}, u32[]{:S(2)}, u32[]{:S(2)}) async-start(bf16[4,448,512]{2,1,0:T(8,128)(2,1)} %broadcast_in_dim.18), calls=%async_computation.2 | async-start | bytes 3670016 | tf_op jit(solution)/shard_map/all_to_all | solution.py:43
  52.4 31.2 %copy-start.7 = (f32[8,1792]{1,0:T(8,128)S(1)}, f32[8,1792]{1,0:T(8,128)}, u32[]{:S(2)}) copy-start(f32[8,1792]{1,0:T(8,128)} %param.13) | copy-start | bytes 172036
  52.4 22.9 %collective-permute-start.3 = (bf16[2,2,112,384]{3,2,1,0:T(8,128)(2,1)S(1)}, bf16[2,2,112,384]{3,2,1,0:T(8,128)(2,1)S(1)}, u32[]{:S(2)}, u32[]{:S(2)}) collective-permute-start(bf16[2,2,112,384]{3,2,1,0:T(8,128)(2,1)S(1)} %pad_maximum_fusion.2), channel_id=1, source_target_pairs={{0,2},{2,4},{4,6},{6,8},{8,10},{10,12},{12,14},{14,0},{1,3},{3,5},... | collective-permute-start | bytes 1032200 | tf_op jit(solution)/shard_map/ppermute | solution.py:39
  55.7 19.7 %collective-permute-start.4 = (bf16[2,2,112,384]{3,2,1,0:T(8,128)(2,1)S(1)}, bf16[2,2,112,384]{3,2,1,0:T(8,128)(2,1)S(1)}, u32[]{:S(2)}, u32[]{:S(2)}) collective-permute-start(bf16[2,2,112,384]{3,2,1,0:T(8,128)(2,1)S(1)} %pad_maximum_fusion.2), channel_id=1, source_target_pairs={{0,14},{2,0},{4,2},{6,4},{8,6},{10,8},{12,10},{14,12},{1,15},{3,1}... | collective-permute-start | bytes 1032200 | tf_op jit(solution)/shard_map/ppermute | solution.py:39
  60.6 12.3 %collective-permute-start.1 = (bf16[2,112,384]{2,1,0:T(8,128)(2,1)S(1)}, bf16[2,112,384]{2,1,0:T(8,128)(2,1)S(1)}, u32[]{:S(2)}, u32[]{:S(2)}) collective-permute-start(bf16[2,112,384]{2,1,0:T(8,128)(2,1)S(1)} %pad_maximum_fusion.3.refs_1_), channel_id=1, source_target_pairs={{0,4},{2,6},{4,8},{6,10},{8,12},{10,14},{12,0},{14,2},{1,5},{3,7},... | collective-permute-start | bytes 516104 | tf_op jit(solution)/shard_map/ppermute | solution.py:39
  63.1 12.2 %collective-permute-start.2 = (bf16[2,112,384]{2,1,0:T(8,128)(2,1)S(1)}, bf16[2,112,384]{2,1,0:T(8,128)(2,1)S(1)}, u32[]{:S(2)}, u32[]{:S(2)}) collective-permute-start(bf16[2,112,384]{2,1,0:T(8,128)(2,1)S(1)} %pad_maximum_fusion.3.refs_1_), channel_id=1, source_target_pairs={{0,12},{2,14},{4,0},{6,2},{8,4},{10,6},{12,8},{14,10},{1,13},{3,15... | collective-permute-start | bytes 516104 | tf_op jit(solution)/shard_map/ppermute | solution.py:39
  75.4 10.9 %collective-permute-start.5 = (bf16[8,2,112,384]{3,2,1,0:T(8,128)(2,1)S(1)}, bf16[8,2,112,384]{3,2,1,0:T(8,128)(2,1)S(1)}, u32[]{:S(2)}, u32[]{:S(2)}) collective-permute-start(bf16[8,2,112,384]{3,2,1,0:T(8,128)(2,1)S(1)} %place.1), channel_id=1, source_target_pairs={{0,1},{1,0},{2,3},{3,2},{4,5},{5,4},{6,7},{7,6},{8,9},{9,8},{10,11... | collective-permute-start | bytes 4128776 | tf_op jit(solution)/shard_map/ppermute | solution.py:39
  93.5 0.8 copy-start.1
  95.3 22.5 %all-to-all-start.3 = ((f32[32,8,512]{2,1,0:T(8,128)}), f32[32,8,512]{2,1,0:T(8,128)S(1)}, u32[]{:S(2)}, u32[]{:S(2)}) async-start(f32[32,8,512]{2,1,0:T(8,128)} %broadcast_in_dim.19), calls=%async_computation.4 | async-start | bytes 1048576 | tf_op jit(solution)/shard_map/all_to_all | solution.py:43
  101.3 76.5 %reduce-scatter.2.cloned.1.call-start = ((), (), s32[]{:S(2)}) async-start(), calls=%async_computation.9 | async-start | bytes 2924544 | tf_op jit(solution)/shard_map/reduce_scatter | solution.py:243
  103.0 2.0 %copy-start.9 = (bf16[1792,1024]{1,0:T(8,128)(2,1)S(1)}, bf16[1792,1024]{1,0:T(8,128)(2,1)}, u32[]{:S(2)}) copy-start(bf16[1792,1024]{1,0:T(8,128)(2,1)} %all-gather.2.cloned.1.call-done) | copy-start | bytes 11010052
  118.5 3.4 %copy-start = (bf16[1,512,1792]{2,1,0:T(8,128)(2,1)S(1)}, bf16[1,512,1792]{2,1,0:T(8,128)(2,1)}, u32[]{:S(2)}) copy-start(bf16[1,512,1792]{2,1,0:T(8,128)(2,1)} %param.12) | copy-start | bytes 5505028
  121.8 1.0 copy-start.4
  123.7 21.7 %all-to-all-start.4 = ((f32[16,8,640]{2,1,0:T(8,128)}), f32[16,8,640]{2,1,0:T(8,128)S(1)}, u32[]{:S(2)}, u32[]{:S(2)}) async-start(f32[16,8,640]{2,1,0:T(8,128)} %select_maximum_fusion), calls=%async_computation.5 | async-start | bytes 655360 | tf_op jit(solution)/shard_map/all_to_all | solution.py:43
  146.1 14.1 %all-to-all-start.5 = ((f32[32,8,128]{2,1,0:T(8,128)}), f32[32,8,128]{2,1,0:T(8,128)S(1)}, u32[]{:S(2)}, u32[]{:S(2)}) async-start(f32[32,8,128]{2,1,0:T(8,128)} %broadcast_in_dim.21), calls=%async_computation.6 | async-start | bytes 262144 | tf_op jit(solution)/shard_map/all_to_all | solution.py:43
  161.0 12.8 %all-to-all-start.6 = ((f32[16,8,128]{2,1,0:T(8,128)}), f32[16,8,128]{2,1,0:T(8,128)S(1)}, u32[]{:S(2)}, u32[]{:S(2)}) async-start(f32[16,8,128]{2,1,0:T(8,128)} %broadcast_in_dim.22), calls=%async_computation.7 | async-start | bytes 131072 | tf_op jit(solution)/shard_map/all_to_all | solution.py:43
  173.7 4.0 %copy-start.2 = (f32[8,1792]{1,0:T(8,128)}, f32[8,1792]{1,0:T(8,128)S(1)}, u32[]{:S(2)}) copy-start(f32[8,1792]{1,0:T(8,128)S(1)} %get-tuple-element.28) | copy-start | bytes 172036
Sparse Core Ops, SparseCore 0:
  21.3 60.6 all-gather.1
  108.9 63.6 reduce-scatter.1

commit v3 on v2

--- a/solution.py
+++ b/solution.py
@@ -92,49 +92,92 @@
     )(at.astype(jnp.int32).reshape(1), *blocks)
 
 
-def orth_kernel(mine, parts, orth, transform, rows):
-    blocks, _, width = parts.shape
-    width = width - LANES
-    for t in range(blocks):
-        rows[:, t * width : (t + 1) * width] = parts[t, :, LANES:]
+def triangle_kernel(p_sum, _, out):
+    rows = p_sum[...]
+    number = lax.broadcasted_iota(jnp.int32, (RANK, 1), 0)
+    lane = lax.broadcasted_iota(jnp.int32, (RANK, LANES), 1)
+    factor = jnp.zeros((RANK, LANES), f32)
+    for j in range(RANK):
+        row = rows[j : j + 1, :]
+        products = jnp.sum(rows * row, axis=1, keepdims=True)
+        length = jnp.sqrt(products[j : j + 1, :])
+        some = length > 0.0
+        scale = jnp.where(some, 1.0 / jnp.where(some, length, 1.0), 0.0)
+        unit = row * scale
+        weight = jnp.where(number > j, products * scale, 0.0)
+        column = jnp.where(number == j, length, weight)
+        factor = jnp.where(lane == j, column, factor)
+        rows = rows - weight * unit
+    out[...] = factor
+
+
+def triangle(p_sum, later):
+    return pl.pallas_call(
+        triangle_kernel,
+        out_shape=jax.ShapeDtypeStruct((RANK, LANES), f32),
+        in_specs=[pl.BlockSpec(memory_space=pltpu.VMEM), pl.BlockSpec(memory_space=pl.ANY)],
+        out_specs=pl.BlockSpec(memory_space=pltpu.VMEM),
+        name="triangle",
+    )(p_sum, later)
+
+
+def split3(value):
+    first = value.astype(bf16)
+    rest = value - first.astype(f32)
+    second = rest.astype(bf16)
+    third = (rest - second.astype(f32)).astype(bf16)
+    return first, second, third
+
+
+def finish_kernel(parts, p_sum, q_avg, left, right):
+    blocks = parts.shape[0]
+    tiles = q_avg.shape[1] // LANES
+    rows = [parts[t, :, LANES:] for t in range(blocks)]
     number = lax.broadcasted_iota(jnp.int32, (RANK, 1), 0)
     column = lax.broadcasted_iota(jnp.int32, (RANK, LANES), 1)
     trans = jnp.where(column == number, 1.0, 0.0).astype(f32)
     for j in range(RANK):
-        whole = rows[...]
-        row = whole[j : j + 1, :]
-        products = jnp.sum(whole * row, axis=1, keepdims=True)
+        each = [block * block[j : j + 1, :] for block in rows]
+        while len(each) > 1:
+            each = [one + two for one, two in zip(each[::2], each[1::2])]
+        products = jnp.sum(each[0], axis=1, keepdims=True)
         length = jnp.sqrt(products[j : j + 1, :])
-        unit = row / length
         weight = jnp.where(number > j, products / length, 0.0)
-        rows[...] = jnp.where(number == j, unit, whole - weight * unit)
-        unit_trans = trans[j : j + 1, :] / length
-        trans = jnp.where(number == j, unit_trans, trans - weight * unit_trans)
-    transform[...] = trans
-    at = pl.multiple_of(mine[0] * width, LANES)
-    orth[...] = rows[:, pl.ds(at, width)]
-
-
-def orthonormal(parts, mine):
-    blocks, _, width = parts.shape
-    width = width - LANES
+        rows = [block - weight * (block[j : j + 1, :] / length) for block in rows]
+        unit = trans[j : j + 1, :] / length
+        trans = jnp.where(number == j, unit, trans - weight * unit)
+
+    def apply(value):
+        total = trans[:, 0:1] * value[0:1, :]
+        for i in range(1, RANK):
+            total = total + trans[:, i : i + 1] * value[i : i + 1, :]
+        return total
+
+    l1, l2, l3 = split3(apply(p_sum[...]))
+    for at, piece in enumerate((l1, l1, l2, l2, l1, l3)):
+        left[at] = piece
+    for t in range(tiles):
+        here = slice(t * LANES, (t + 1) * LANES)
+        average = apply(parts[t, :, :LANES]) / (Z * X)
+        q_avg[:, here] = average
+        r1, r2, r3 = split3(average)
+        for at, piece in enumerate((r1, r2, r1, r2, r3, r1)):
+            right[at, :, here] = piece
+
+
+def finish(parts, p_sum, width):
     return pl.pallas_call(
-        orth_kernel,
+        finish_kernel,
         out_shape=(
             jax.ShapeDtypeStruct((RANK, width), f32),
-            jax.ShapeDtypeStruct((RANK, LANES), f32),
+            jax.ShapeDtypeStruct((6, RANK, p_sum.shape[1]), bf16),
+            jax.ShapeDtypeStruct((6, RANK, width), bf16),
         ),
-        in_specs=[
-            pl.BlockSpec(memory_space=pltpu.SMEM),
-            pl.BlockSpec(memory_space=pltpu.VMEM),
-        ],
-        out_specs=(
-            pl.BlockSpec(memory_space=pltpu.VMEM),
-            pl.BlockSpec(memory_space=pltpu.VMEM),
+        cost_estimate=pl.CostEstimate(
+            flops=40_000_000_000, bytes_accessed=130_000_000, transcendentals=0
         ),
-        scratch_shapes=[pltpu.VMEM((RANK, blocks * width), f32)],
-        compiler_params=pltpu.CompilerParams(vmem_limit_bytes=16 * 1024 * 1024),
-    )(mine, parts)
+        name="finish",
+    )(parts, p_sum)
 
 
 def grad_share(d_hidden, up_val, slope, active, weights):
@@ -142,20 +185,6 @@
     d_up = (d_hidden * active).astype(bf16)
     grads = contract(weights, jnp.concatenate([d_gate, d_up]), 1, 0)
     return grads
-
-
-def pass_kernel(value, _, out):
-    out[...] = value[...]
-
-
-def when_ready(value, other):
-    return pl.pallas_call(
-        pass_kernel,
-        out_shape=jax.ShapeDtypeStruct(value.shape, value.dtype),
-        in_specs=[pl.BlockSpec(memory_space=pltpu.VMEM), pl.BlockSpec(memory_space=pl.ANY)],
-        out_specs=pl.BlockSpec(memory_space=pltpu.VMEM),
-        name="when_ready",
-    )(value, other)
 
 
 def per_device(tokens, cotangent, gate_weight, up_weight, down_weight, error_buffer, q_init):
@@ -211,7 +240,8 @@
     p_part = fold3(contract(cot_q, hidden, 1, 1)) + err_q
     p_all = gather(p_part, ("z", "x"))
     grads = grad_share(d_hidden, up_val, slope, active, weights)
-    p_sum = when_ready(jnp.sum(p_all, axis=0), grads)
+    p_all, shares = lax.optimization_barrier((p_all, grads))
+    p_sum = jnp.sum(p_all, axis=0)
 
     p_stack = stack3(p_sum)
     hid_p = stack3(fold3(contract(p_stack, hidden, 1, 0)))
@@ -219,23 +249,12 @@
     tiles = q_part.reshape(RANK, -1, LANES).transpose(1, 0, 2)
     n_tiles = tiles.shape[0]
     tiles = jnp.concatenate([tiles, jnp.zeros((Y * C - n_tiles,) + tiles.shape[1:], f32)])
-    message = jnp.concatenate(
-        [tiles, jnp.broadcast_to(p_sum[None], (Y * C,) + p_sum.shape)], axis=2
-    )
-    parts = swap(message, ("y", "c"))
-    q_tile = jnp.sum(parts[:, :, :LANES], axis=0)
-    p_orth, trans = orthonormal(parts, (y_at * C + c_at).astype(jnp.int32).reshape(1))
+    q_tile = jnp.sum(swap(tiles, ("y", "c")), axis=0)
     q_tile = jnp.sum(gather(q_tile, ("z", "x")), axis=0)
-    q_tile = jnp.dot(trans[:, :RANK], q_tile, precision=lax.Precision.HIGHEST) / (Z * X)
-    q_avg = gather(q_tile, ("y", "c"))[:n_tiles].transpose(1, 0, 2).reshape(RANK, -1)
-
-    p1, p2, p3 = pieces(p_orth)
-    q1, q2, q3 = pieces(q_avg)
-    approx = contract(
-        jnp.concatenate([p1, p1, p2, p2, p1, p3]),
-        jnp.concatenate([q1, q2, q1, q2, q3, q1]),
-        0,
-        0,
+    ends = gather(jnp.concatenate([q_tile, triangle(p_sum, shares)], axis=1), ("y", "c"))
+    q_avg, left, right = finish(ends, p_sum, errors.shape[1])
+    approx = lax.dot_general(
+        left, right, (((0, 1), (0, 1)), ((), ())), preferred_element_type=f32
     )
     local_grad = contract(hidden, upstream, 1, 1)
     new_error = (local_grad + errors.astype(f32) - approx).astype(bf16)[None]

time: 187 us -> 183 us (0.979)
  blocking collectives: 0 us -> 29.3 us
  waiting for transfers between devices: 56.8 us -> 37.6 us
  starting transfers between devices: 73.4 us -> 61.8 us
  matrix products: 22.5 us -> 18.6 us
    all_to_all x0 -> x2, blocking collectives: none -> 29.3 us  [swap(): return lax.all_to_all(stacked, axes, 0, 0, tiled=True)]
    all_to_all x7 -> x5, waiting for transfers between devices: 46 us -> 26.7 us  [swap(): return lax.all_to_all(stacked, axes, 0, 0, tiled=True)]
    all_to_all x7 -> x5, starting transfers between devices: 42.3 us -> 30.6 us  [swap(): return lax.all_to_all(stacked, axes, 0, 0, tiled=True)]
    dot_general x11 -> x10, matrix products: 22.3 us -> 16.9 us  [contract(): lax.dot_general(left, right, (((dim_left,), (dim_right,)), ((), ())), pre...]
  transfers between devices with their start and end apart: 15 -> 13, of which waited for: 10 -> 8; matrix products, arithmetic and copies ran while one was open for 15% -> 12% of each run, Pallas kernels for 2% -> 3%
where the time goes in v3:
time: 183 us; the launch traced here: 181 us
  starting transfers between devices  61.8 us (34%)
  waiting for transfers between devices  37.6 us (21%)
  blocking collectives  29.3 us (16%)
  matrix products  18.6 us (10%)
  between operations  14.4 us (8%)
  local copies, waits for them, and re-layouts  8.54 us (5%)
  other arithmetic  6.41 us (4%)
  Pallas kernels  4.83 us (3%)
    ppermute x6, starting transfers between devices, shift(): return lax.ppermute(value, axis, [(i, (i + step) % n) for i in range(n)])  31.1 us
    all_to_all x5, starting transfers between devices, swap(): return lax.all_to_all(stacked, axes, 0, 0, tiled=True)  30.6 us
    all_to_all x2, blocking collectives, swap(): return lax.all_to_all(stacked, axes, 0, 0, tiled=True)  29.3 us
    all_to_all x5, waiting for transfers between devices, swap(): return lax.all_to_all(stacked, axes, 0, 0, tiled=True)  26.7 us
    dot_general x10, matrix products, contract(): lax.dot_general(left, right, (((dim_left,), (dim_right,)), ((), ())), pre...  16.9 us
    ppermute x6, waiting for transfers between devices, shift(): return lax.ppermute(value, axis, [(i, (i + step) % n) for i in range(n)])  10.8 us
    broadcast_in_dim x6, local copies, waits for them, and re-layouts, gather(): return swap(jnp.broadcast_to(value[None], (n,) + value.shape), axes)  4.53 us
  transfers between devices with their start and end apart: 13, of which 8 were waited for; matrix products, arithmetic and copies ran while one was open for 12% of the time, Pallas kernels for 3%

profile of v3, /device:TPU:1, one launch (start us, length us, event | category | flops | bytes accessed | tf_op | source)
XLA Modules:
  0.0 181.3 jit_solution(8616270750470984214)
XLA Ops:
  7.2 0.9 pad_maximum_fusion.4
  8.1 0.8 broadcast_in_dim.14
  8.9 4.8 %all-to-all-start = ((bf16[4,56,1024]{2,1,0:T(8,128)(2,1)}), bf16[4,56,1024]{2,1,0:T(8,128)(2,1)S(1)}, u32[]{:S(2)}, u32[]{:S(2)}) async-start(bf16[4,56,1024]{2,1,0:T(8,128)(2,1)} %broadcast_in_dim.14), calls=%async_computation | async-start | bytes 917504 | tf_op jit(solution)/shard_map/all_to_all | solution.py:43
  13.8 6.5 %all-to-all-done = bf16[4,56,1024]{2,1,0:T(8,128)(2,1)S(1)} async-done(((bf16[4,56,1024]{2,1,0:T(8,128)(2,1)}), bf16[4,56,1024]{2,1,0:T(8,128)(2,1)S(1)}, u32[]{:S(2)}, u32[]{:S(2)}) %all-to-all-start) | async-done | bytes 458784 | tf_op jit(solution)/shard_map/all_to_all | solution.py:43
  20.3 0.8 copy-done.3
  21.1 0.8 broadcast_in_dim.15
  21.9 11.0 %all-to-all-start.1 = ((bf16[8,56,512]{2,1,0:T(8,128)(2,1)}), bf16[8,56,512]{2,1,0:T(8,128)(2,1)S(1)}, u32[]{:S(2)}, u32[]{:S(2)}) async-start(bf16[8,56,512]{2,1,0:T(8,128)(2,1)} %broadcast_in_dim.15), calls=%async_computation.1 | async-start | bytes 917504 | tf_op jit(solution)/shard_map/all_to_all | solution.py:43
  33.0 7.4 %collective-permute-start = (bf16[2,112,384]{2,1,0:T(8,128)(2,1)S(1)}, bf16[2,112,384]{2,1,0:T(8,128)(2,1)S(1)}, u32[]{:S(2)}, u32[]{:S(2)}) collective-permute-start(bf16[2,112,384]{2,1,0:T(8,128)(2,1)S(1)} %pad_maximum_fusion.3.refs_1_), channel_id=1, source_target_pairs={{0,8},{2,10},{4,12},{6,14},{8,0},{10,2},{12,4},{14,6},{1,9},{3,11}... | collective-permute-start | bytes 516104 | tf_op jit(solution)/shard_map/ppermute | solution.py:39
  40.4 2.9 %collective-permute-done.refs_2_ = bf16[2,112,384]{2,1,0:T(8,128)(2,1)S(1)} collective-permute-done((bf16[2,112,384]{2,1,0:T(8,128)(2,1)S(1)}, bf16[2,112,384]{2,1,0:T(8,128)(2,1)S(1)}, u32[]{:S(2)}, u32[]{:S(2)}) %collective-permute-start) | collective-permute-done | bytes 172064 | tf_op jit(solution)/shard_map/ppermute | solution.py:39
  43.3 3.3 %all-to-all-done.1 = bf16[8,56,512]{2,1,0:T(8,128)(2,1)S(1)} async-done(((bf16[8,56,512]{2,1,0:T(8,128)(2,1)}), bf16[8,56,512]{2,1,0:T(8,128)(2,1)S(1)}, u32[]{:S(2)}, u32[]{:S(2)}) %all-to-all-start.1) | async-done | bytes 458784 | tf_op jit(solution)/shard_map/all_to_all | solution.py:43
  46.6 1.4 broadcast_in_dim.16
  48.0 4.4 %all-to-all-start.2 = ((bf16[4,448,512]{2,1,0:T(8,128)(2,1)}), bf16[4,448,512]{2,1,0:T(8,128)(2,1)}, u32[]{:S(2)}, u32[]{:S(2)}) async-start(bf16[4,448,512]{2,1,0:T(8,128)(2,1)} %broadcast_in_dim.16), calls=%async_computation.2 | async-start | bytes 3670016 | tf_op jit(solution)/shard_map/all_to_all | solution.py:43
  52.4 3.2 %collective-permute-start.3 = (bf16[2,2,112,384]{3,2,1,0:T(8,128)(2,1)S(1)}, bf16[2,2,112,384]{3,2,1,0:T(8,128)(2,1)S(1)}, u32[]{:S(2)}, u32[]{:S(2)}) collective-permute-start(bf16[2,2,112,384]{3,2,1,0:T(8,128)(2,1)S(1)} %pad_maximum_fusion.2), channel_id=1, source_target_pairs={{0,2},{2,4},{4,6},{6,8},{8,10},{10,12},{12,14},{14,0},{1,3},{3,5},... | collective-permute-start | bytes 1032200 | tf_op jit(solution)/shard_map/ppermute | solution.py:39
  55.6 4.9 %collective-permute-start.4 = (bf16[2,2,112,384]{3,2,1,0:T(8,128)(2,1)S(1)}, bf16[2,2,112,384]{3,2,1,0:T(8,128)(2,1)S(1)}, u32[]{:S(2)}, u32[]{:S(2)}) collective-permute-start(bf16[2,2,112,384]{3,2,1,0:T(8,128)(2,1)S(1)} %pad_maximum_fusion.2), channel_id=1, source_target_pairs={{0,14},{2,0},{4,2},{6,4},{8,6},{10,8},{12,10},{14,12},{1,15},{3,1}... | collective-permute-start | bytes 1032200 | tf_op jit(solution)/shard_map/ppermute | solution.py:39
  60.6 2.5 %collective-permute-start.1 = (bf16[2,112,384]{2,1,0:T(8,128)(2,1)S(1)}, bf16[2,112,384]{2,1,0:T(8,128)(2,1)S(1)}, u32[]{:S(2)}, u32[]{:S(2)}) collective-permute-start(bf16[2,112,384]{2,1,0:T(8,128)(2,1)S(1)} %pad_maximum_fusion.3.refs_1_), channel_id=1, source_target_pairs={{0,4},{2,6},{4,8},{6,10},{8,12},{10,14},{12,0},{14,2},{1,5},{3,7},... | collective-permute-start | bytes 516104 | tf_op jit(solution)/shard_map/ppermute | solution.py:39
  63.1 4.9 %collective-permute-start.2 = (bf16[2,112,384]{2,1,0:T(8,128)(2,1)S(1)}, bf16[2,112,384]{2,1,0:T(8,128)(2,1)S(1)}, u32[]{:S(2)}, u32[]{:S(2)}) collective-permute-start(bf16[2,112,384]{2,1,0:T(8,128)(2,1)S(1)} %pad_maximum_fusion.3.refs_1_), channel_id=1, source_target_pairs={{0,12},{2,14},{4,0},{6,2},{8,4},{10,6},{12,8},{14,10},{1,13},{3,15... | collective-permute-start | bytes 516104 | tf_op jit(solution)/shard_map/ppermute | solution.py:39
  68.0 4.9 %collective-permute-done.1.refs_3_ = bf16[2,112,384]{2,1,0:T(8,128)(2,1)S(1)} collective-permute-done((bf16[2,112,384]{2,1,0:T(8,128)(2,1)S(1)}, bf16[2,112,384]{2,1,0:T(8,128)(2,1)S(1)}, u32[]{:S(2)}, u32[]{:S(2)}) %collective-permute-start.1) | collective-permute-done | bytes 172064 | tf_op jit(solution)/shard_map/ppermute | solution.py:39
  72.9 2.4 %collective-permute-done.2.refs_4_ = bf16[2,112,384]{2,1,0:T(8,128)(2,1)S(1)} collective-permute-done((bf16[2,112,384]{2,1,0:T(8,128)(2,1)S(1)}, bf16[2,112,384]{2,1,0:T(8,128)(2,1)S(1)}, u32[]{:S(2)}, u32[]{:S(2)}) %collective-permute-start.2) | collective-permute-done | bytes 172064 | tf_op jit(solution)/shard_map/ppermute | solution.py:39
  75.4 8.1 %collective-permute-start.5 = (bf16[8,2,112,384]{3,2,1,0:T(8,128)(2,1)S(1)}, bf16[8,2,112,384]{3,2,1,0:T(8,128)(2,1)S(1)}, u32[]{:S(2)}, u32[]{:S(2)}) collective-permute-start(bf16[8,2,112,384]{3,2,1,0:T(8,128)(2,1)S(1)} %place.1), channel_id=1, source_target_pairs={{0,1},{1,0},{2,3},{3,2},{4,5},{5,4},{6,7},{7,6},{8,9},{9,8},{10,11... | collective-permute-start | bytes 4128776 | tf_op jit(solution)/shard_map/ppermute | solution.py:39
  83.6 2.1 %fusion.4 = f32[24,512]{1,0:T(8,128)S(1)} fusion(bf16[1,512,1792]{2,1,0:T(8,128)(2,1)} %param.12, bf16[8,1792]{1,0:T(8,128)(2,1)S(1)} %get-tuple-element.46, bf16[8,1792]{1,0:T(8,128)(2,1)S(1)} %get-tuple-element.47, bf16[8,1792]{1,0:T(8,128)(2,1)S(1)} %get-tuple-element.45), kind=kOutput, calls=%fused_computation.5 | convolution fusion | flops 44298240 | bytes 1970176 | tf_op jit(solution)/shard_map/dot_general | solution.py:32
  85.7 0.6 collective-permute-done.5
  86.8 1.2 pad_maximum_fusion
  88.2 0.3 fusion.22
  88.6 4.5 %fusion.55 = f32[1024,384]{1,0:T(8,128)S(1)} fusion(bf16[1792,1024]{1,0:T(8,128)(2,1)} %all-gather.2.cloned.1.call-done, bf16[1792,384]{1,0:T(8,128)(2,1)} %bitcast.60), kind=kOutput, calls=%fused_computation.92 | convolution fusion | flops 1409286144 | bytes 6619136 | tf_op jit(solution)/shard_map/dot_general | solution.py:32
  93.1 0.3 multiply_convert_fusion.1
  93.4 0.8 copy-done.1
  94.5 0.9 broadcast_in_dim.17
  95.3 6.0 %all-to-all-start.3 = ((f32[32,8,512]{2,1,0:T(8,128)}), f32[32,8,512]{2,1,0:T(8,128)}, u32[]{:S(2)}, u32[]{:S(2)}) async-start(f32[32,8,512]{2,1,0:T(8,128)} %broadcast_in_dim.17), calls=%async_computation.4 | async-start | bytes 1048576 | tf_op jit(solution)/shard_map/all_to_all | solution.py:43
  101.4 1.7 copy.11
  103.1 1.5 fusion.12
  104.7 0.5 copy-done.9
  105.1 3.6 %fusion.13._ = f32[1792,384]{1,0:T(8,128)} fusion(bf16[1792,1024]{1,0:T(8,128)(2,1)S(1)} %copy-done.9, bf16[512,384]{1,0:T(8,128)(2,1)S(1)} %get-tuple-element.40, bf16[512,384]{1,0:T(8,128)(2,1)S(1)} %get-tuple-element.39), kind=kOutput, calls=%fused_computation.20 | convolution fusion | flops 1410859008 | bytes 7208960 | tf_op jit(solution)/shard_map/dot_general | solution.py:32
  108.8 9.1 %all-to-all-done.3 = f32[32,8,512]{2,1,0:T(8,128)} async-done(((f32[32,8,512]{2,1,0:T(8,128)}), f32[32,8,512]{2,1,0:T(8,128)}, u32[]{:S(2)}, u32[]{:S(2)}) %all-to-all-start.3) | async-done | bytes 524320 | tf_op jit(solution)/shard_map/all_to_all | solution.py:43
  117.9 1.1 reduce_sum.27.p_sum
  119.0 1.2 fusion.43
  120.2 0.4 fusion.2
  120.6 0.6 fusion.29
  121.3 14.9 %all_to_all.35 = f32[16,8,128]{2,1,0:T(8,128)S(1)} all-to-all(f32[16,8,128]{2,1,0:T(8,128)S(1)} %concatenate.30), channel_id=1, replica_groups=mesh['z'=8,'x'=4,'y'=8,'c'=2] {'y','c'}, dimensions={0} | all-to-all | bytes 131072 | tf_op jit(solution)/shard_map/all_to_all | solution.py:43
  136.2 0.7 broadcast_in_dim.18
  136.8 4.3 %all-to-all-start.5 = ((f32[32,8,128]{2,1,0:T(8,128)}), f32[32,8,128]{2,1,0:T(8,128)S(1)}, u32[]{:S(2)}, u32[]{:S(2)}) async-start(f32[32,8,128]{2,1,0:T(8,128)} %broadcast_in_dim.18), calls=%async_computation.6 | async-start | bytes 262144 | tf_op jit(solution)/shard_map/all_to_all | solution.py:43
  141.1 2.1 %triangle.1 = f32[8,128]{1,0:T(8,128)} custom-call(f32[8,512]{1,0:T(8,128)} %copy-done.4, f32[1792,384]{1,0:T(8,128)} %fusion.13._), custom_call_target="tpu_custom_call" | custom-call | tf_op jit(solution)/shard_map/triangle/pallas_call | solution.py:115
  143.2 7.8 %all-to-all-done.5 = f32[32,8,128]{2,1,0:T(8,128)S(1)} async-done(((f32[32,8,128]{2,1,0:T(8,128)}), f32[32,8,128]{2,1,0:T(8,128)S(1)}, u32[]{:S(2)}, u32[]{:S(2)}) %all-to-all-start.5) | async-done | bytes 131104 | tf_op jit(solution)/shard_map/all_to_all | solution.py:43
  151.1 0.7 pad_maximum_fusion.11
  151.8 14.4 %all_to_all.36.parts = f32[16,8,256]{2,1,0:T(8,128)} all-to-all(f32[16,8,256]{2,1,0:T(8,128)S(1)} %broadcast_in_dim.19), channel_id=1, replica_groups=mesh['z'=8,'x'=4,'y'=8,'c'=2] {'y','c'}, dimensions={0} | all-to-all | bytes 262144 | tf_op jit(solution)/shard_map/all_to_all | solution.py:43
  166.2 2.6 %finish.1 = (f32[8,1792]{1,0:T(8,128)}, bf16[6,8,512]{2,1,0:T(8,128)(2,1)}, bf16[6,8,1792]{2,1,0:T(8,128)(2,1)}) custom-call(f32[16,8,256]{2,1,0:T(8,128)} %all_to_all.36.parts, f32[8,512]{1,0:T(8,128)} %copy-done.4), custom_call_target="tpu_custom_call" | custom-call | flops 40000000000 | bytes 130000000 | tf_op jit(solution)/shard_map/finish/pallas_call | solution.py:169
  168.8 1.7 fusion.56
  170.5 2.4 %fusion.1 = bf16[1,512,1792]{2,1,0:T(8,128)(2,1)} fusion(f32[512,1792,1]{1,0,2:T(8,128)S(1)} %fusion.56, bf16[512,384]{1,0:T(8,128)(2,1)S(1)} %copy-done.2, bf16[1792,384]{1,0:T(8,128)(2,1)S(1)} %bitcast.56, bf16[1,512,1792]{2,1,0:T(8,128)(2,1)S(1)} %copy-done), kind=kOutput, calls=%fused_computation.2 | convolution fusion | flops 708313088 | bytes 9109504 | tf_op jit(solution)/shard_map/dot_general | solution.py:32
  172.9 1.6 convert_bitcast_fusion
  (45 shorter events, 1.5 us)
Async XLA Ops:
  7.2 6.6 %copy-start.5 = (bf16[384,112]{0,1:T(8,128)(2,1)S(1)}, bf16[384,112]{0,1:T(8,128)(2,1)}, u32[]{:S(2)}) copy-start(bf16[384,112]{0,1:T(8,128)(2,1)} %param.8) | copy-start | bytes 258052
  7.2 6.6 %copy-start.6 = (bf16[384,112]{0,1:T(8,128)(2,1)S(1)}, bf16[384,112]{0,1:T(8,128)(2,1)}, u32[]{:S(2)}) copy-start(bf16[384,112]{0,1:T(8,128)(2,1)} %param.7) | copy-start | bytes 258052
  7.2 14.0 %copy-start.8 = (bf16[512,56]{0,1:T(8,128)(2,1)S(1)}, bf16[512,56]{0,1:T(8,128)(2,1)}, u32[]{:S(2)}) copy-start(bf16[512,56]{0,1:T(8,128)(2,1)} %param.11) | copy-start | bytes 172036
  8.9 11.4 %all-to-all-start = ((bf16[4,56,1024]{2,1,0:T(8,128)(2,1)}), bf16[4,56,1024]{2,1,0:T(8,128)(2,1)S(1)}, u32[]{:S(2)}, u32[]{:S(2)}) async-start(bf16[4,56,1024]{2,1,0:T(8,128)(2,1)} %broadcast_in_dim.14), calls=%async_computation | async-start | bytes 917504 | tf_op jit(solution)/shard_map/all_to_all | solution.py:43
  13.8 74.8 %all-gather.2.cloned.1.call-start = ((), (), s32[]{:S(2)}) async-start(), calls=%async_computation.8 | async-start | bytes 4128768 | tf_op jit(solution)/shard_map/all_gather | solution.py:204
  20.3 0.8 copy-start.3
  21.9 24.6 %all-to-all-start.1 = ((bf16[8,56,512]{2,1,0:T(8,128)(2,1)}), bf16[8,56,512]{2,1,0:T(8,128)(2,1)S(1)}, u32[]{:S(2)}, u32[]{:S(2)}) async-start(bf16[8,56,512]{2,1,0:T(8,128)(2,1)} %broadcast_in_dim.15), calls=%async_computation.1 | async-start | bytes 917504 | tf_op jit(solution)/shard_map/all_to_all | solution.py:43
  33.0 10.3 %collective-permute-start = (bf16[2,112,384]{2,1,0:T(8,128)(2,1)S(1)}, bf16[2,112,384]{2,1,0:T(8,128)(2,1)S(1)}, u32[]{:S(2)}, u32[]{:S(2)}) collective-permute-start(bf16[2,112,384]{2,1,0:T(8,128)(2,1)S(1)} %pad_maximum_fusion.3.refs_1_), channel_id=1, source_target_pairs={{0,8},{2,10},{4,12},{6,14},{8,0},{10,2},{12,4},{14,6},{1,9},{3,11}... | collective-permute-start | bytes 516104 | tf_op jit(solution)/shard_map/ppermute | solution.py:39
  48.0 27.4 %all-to-all-start.2 = ((bf16[4,448,512]{2,1,0:T(8,128)(2,1)}), bf16[4,448,512]{2,1,0:T(8,128)(2,1)}, u32[]{:S(2)}, u32[]{:S(2)}) async-start(bf16[4,448,512]{2,1,0:T(8,128)(2,1)} %broadcast_in_dim.16), calls=%async_computation.2 | async-start | bytes 3670016 | tf_op jit(solution)/shard_map/all_to_all | solution.py:43
  52.4 31.2 %copy-start.7 = (f32[8,1792]{1,0:T(8,128)S(1)}, f32[8,1792]{1,0:T(8,128)}, u32[]{:S(2)}) copy-start(f32[8,1792]{1,0:T(8,128)} %param.13) | copy-start | bytes 172036
  52.4 22.9 %collective-permute-start.3 = (bf16[2,2,112,384]{3,2,1,0:T(8,128)(2,1)S(1)}, bf16[2,2,112,384]{3,2,1,0:T(8,128)(2,1)S(1)}, u32[]{:S(2)}, u32[]{:S(2)}) collective-permute-start(bf16[2,2,112,384]{3,2,1,0:T(8,128)(2,1)S(1)} %pad_maximum_fusion.2), channel_id=1, source_target_pairs={{0,2},{2,4},{4,6},{6,8},{8,10},{10,12},{12,14},{14,0},{1,3},{3,5},... | collective-permute-start | bytes 1032200 | tf_op jit(solution)/shard_map/ppermute | solution.py:39
  55.6 19.7 %collective-permute-start.4 = (bf16[2,2,112,384]{3,2,1,0:T(8,128)(2,1)S(1)}, bf16[2,2,112,384]{3,2,1,0:T(8,128)(2,1)S(1)}, u32[]{:S(2)}, u32[]{:S(2)}) collective-permute-start(bf16[2,2,112,384]{3,2,1,0:T(8,128)(2,1)S(1)} %pad_maximum_fusion.2), channel_id=1, source_target_pairs={{0,14},{2,0},{4,2},{6,4},{8,6},{10,8},{12,10},{14,12},{1,15},{3,1}... | collective-permute-start | bytes 1032200 | tf_op jit(solution)/shard_map/ppermute | solution.py:39
  60.6 12.3 %collective-permute-start.1 = (bf16[2,112,384]{2,1,0:T(8,128)(2,1)S(1)}, bf16[2,112,384]{2,1,0:T(8,128)(2,1)S(1)}, u32[]{:S(2)}, u32[]{:S(2)}) collective-permute-start(bf16[2,112,384]{2,1,0:T(8,128)(2,1)S(1)} %pad_maximum_fusion.3.refs_1_), channel_id=1, source_target_pairs={{0,4},{2,6},{4,8},{6,10},{8,12},{10,14},{12,0},{14,2},{1,5},{3,7},... | collective-permute-start | bytes 516104 | tf_op jit(solution)/shard_map/ppermute | solution.py:39
  63.1 12.2 %collective-permute-start.2 = (bf16[2,112,384]{2,1,0:T(8,128)(2,1)S(1)}, bf16[2,112,384]{2,1,0:T(8,128)(2,1)S(1)}, u32[]{:S(2)}, u32[]{:S(2)}) collective-permute-start(bf16[2,112,384]{2,1,0:T(8,128)(2,1)S(1)} %pad_maximum_fusion.3.refs_1_), channel_id=1, source_target_pairs={{0,12},{2,14},{4,0},{6,2},{8,4},{10,6},{12,8},{14,10},{1,13},{3,15... | collective-permute-start | bytes 516104 | tf_op jit(solution)/shard_map/ppermute | solution.py:39
  75.4 10.9 %collective-permute-start.5 = (bf16[8,2,112,384]{3,2,1,0:T(8,128)(2,1)S(1)}, bf16[8,2,112,384]{3,2,1,0:T(8,128)(2,1)S(1)}, u32[]{:S(2)}, u32[]{:S(2)}) collective-permute-start(bf16[8,2,112,384]{3,2,1,0:T(8,128)(2,1)S(1)} %place.1), channel_id=1, source_target_pairs={{0,1},{1,0},{2,3},{3,2},{4,5},{5,4},{6,7},{7,6},{8,9},{9,8},{10,11... | collective-permute-start | bytes 4128776 | tf_op jit(solution)/shard_map/ppermute | solution.py:39
  93.4 0.8 copy-start.1
  95.3 22.6 %all-to-all-start.3 = ((f32[32,8,512]{2,1,0:T(8,128)}), f32[32,8,512]{2,1,0:T(8,128)}, u32[]{:S(2)}, u32[]{:S(2)}) async-start(f32[32,8,512]{2,1,0:T(8,128)} %broadcast_in_dim.17), calls=%async_computation.4 | async-start | bytes 1048576 | tf_op jit(solution)/shard_map/all_to_all | solution.py:43
  101.4 71.6 %reduce-scatter.2.cloned.1.call-start = ((), (), s32[]{:S(2)}) async-start(), calls=%async_computation.9 | async-start | bytes 2924544 | tf_op jit(solution)/shard_map/reduce_scatter | solution.py:262
  103.1 2.0 %copy-start.9 = (bf16[1792,1024]{1,0:T(8,128)(2,1)S(1)}, bf16[1792,1024]{1,0:T(8,128)(2,1)}, u32[]{:S(2)}) copy-start(bf16[1792,1024]{1,0:T(8,128)(2,1)} %all-gather.2.cloned.1.call-done) | copy-start | bytes 11010052
  108.8 11.4 %copy-start = (bf16[1,512,1792]{2,1,0:T(8,128)(2,1)S(1)}, bf16[1,512,1792]{2,1,0:T(8,128)(2,1)}, u32[]{:S(2)}) copy-start(bf16[1,512,1792]{2,1,0:T(8,128)(2,1)} %param.12) | copy-start | bytes 5505028
  119.0 2.2 %copy-start.4 = (f32[8,512]{1,0:T(8,128)}, f32[8,512]{1,0:T(8,128)S(1)}, u32[]{:S(2)}) copy-start(f32[8,512]{1,0:T(8,128)S(1)} %reduce_sum.27.p_sum) | copy-start | bytes 49156
  136.8 14.2 %all-to-all-start.5 = ((f32[32,8,128]{2,1,0:T(8,128)}), f32[32,8,128]{2,1,0:T(8,128)S(1)}, u32[]{:S(2)}, u32[]{:S(2)}) async-start(f32[32,8,128]{2,1,0:T(8,128)} %broadcast_in_dim.18), calls=%async_computation.6 | async-start | bytes 262144 | tf_op jit(solution)/shard_map/all_to_all | solution.py:43
  168.8 1.7 copy-start.2
Sparse Core Ops, SparseCore 0:
  21.3 60.6 all-gather.1
  108.9 62.0 reduce-scatter.1

commit v4 on v3

--- a/solution.py
+++ b/solution.py
@@ -207,7 +207,7 @@
     far = shift(block, "y", 4)
     back2 = shift(block, "y", 2)
     fore2 = shift(block, "y", -2)
-    down_z, block, far = lax.optimization_barrier((down_z, block, far))
+    down_z, block, far, back2, fore2 = lax.optimization_barrier((down_z, block, far, back2, fore2))
     down_all = gather(down_z, ("x",))
     both = jnp.stack([block, far])
     back = shift(both, "y", 1)
@@ -218,7 +218,6 @@
         Y,
         y_at,
     )
-    mine, down_all = lax.optimization_barrier((mine, down_all))
     other = shift(mine, "c", 1)
     even = jnp.where(first, mine, other)
     odd = jnp.where(first, other, mine)

time: 183 us -> 197 us (1.077)
  waiting for transfers between devices: 37.6 us -> 53.4 us
  starting transfers between devices: 61.8 us -> 57.3 us
    all_to_all x5, waiting for transfers between devices: 26.7 us -> 37.5 us  [swap(): return lax.all_to_all(stacked, axes, 0, 0, tiled=True)]
    ppermute x6, starting transfers between devices: 31.1 us -> 24.9 us  [shift(): return lax.ppermute(value, axis, [(i, (i + step) % n) for i in range(n)])]
    ppermute x6, waiting for transfers between devices: 10.8 us -> 15.9 us  [shift(): return lax.ppermute(value, axis, [(i, (i + step) % n) for i in range(n)])]
  transfers between devices with their start and end apart: 13 -> 13, of which waited for: 8 -> 8; matrix products, arithmetic and copies ran while one was open for 12% -> 15% of each run, Pallas kernels for 3% -> 2%
where the time goes in v4:
time: 197 us; the launch traced here: 195 us
  starting transfers between devices  57.3 us (29%)
  waiting for transfers between devices  53.4 us (27%)
  blocking collectives  31.1 us (16%)
  matrix products  18.6 us (9%)
  between operations  14.4 us (7%)
  other arithmetic  7.81 us (4%)
  local copies, waits for them, and re-layouts  7.8 us (4%)
  Pallas kernels  4.83 us (2%)
    all_to_all x5, waiting for transfers between devices, swap(): return lax.all_to_all(stacked, axes, 0, 0, tiled=True)  37.5 us
    all_to_all x5, starting transfers between devices, swap(): return lax.all_to_all(stacked, axes, 0, 0, tiled=True)  32.4 us
    all_to_all x2, blocking collectives, swap(): return lax.all_to_all(stacked, axes, 0, 0, tiled=True)  31.1 us
    ppermute x6, starting transfers between devices, shift(): return lax.ppermute(value, axis, [(i, (i + step) % n) for i in range(n)])  24.9 us
    dot_general x10, matrix products, contract(): lax.dot_general(left, right, (((dim_left,), (dim_right,)), ((), ())), pre...  16.9 us
    ppermute x6, waiting for transfers between devices, shift(): return lax.ppermute(value, axis, [(i, (i + step) % n) for i in range(n)])  15.9 us
    broadcast_in_dim x6, local copies, waits for them, and re-layouts, gather(): return swap(jnp.broadcast_to(value[None], (n,) + value.shape), axes)  4.55 us
  transfers between devices with their start and end apart: 13, of which 8 were waited for; matrix products, arithmetic and copies ran while one was open for 15% of the time, Pallas kernels for 2%

profile of v4, /device:TPU:1, one launch (start us, length us, event | category | flops | bytes accessed | tf_op | source)
XLA Modules:
  0.0 195.2 jit_solution(7634213839343303313)
XLA Ops:
  7.2 0.9 pad_maximum_fusion.4
  8.1 0.8 broadcast_in_dim.14
  8.9 4.8 %all-to-all-start = ((bf16[4,56,1024]{2,1,0:T(8,128)(2,1)}), bf16[4,56,1024]{2,1,0:T(8,128)(2,1)S(1)}, u32[]{:S(2)}, u32[]{:S(2)}) async-start(bf16[4,56,1024]{2,1,0:T(8,128)(2,1)} %broadcast_in_dim.14), calls=%async_computation | async-start | bytes 917504 | tf_op jit(solution)/shard_map/all_to_all | solution.py:43
  13.8 6.5 %all-to-all-done = bf16[4,56,1024]{2,1,0:T(8,128)(2,1)S(1)} async-done(((bf16[4,56,1024]{2,1,0:T(8,128)(2,1)}), bf16[4,56,1024]{2,1,0:T(8,128)(2,1)S(1)}, u32[]{:S(2)}, u32[]{:S(2)}) %all-to-all-start) | async-done | bytes 458784 | tf_op jit(solution)/shard_map/all_to_all | solution.py:43
  20.3 0.8 copy-done.3
  21.2 0.8 broadcast_in_dim.15
  22.0 11.0 %all-to-all-start.1 = ((bf16[8,56,512]{2,1,0:T(8,128)(2,1)}), bf16[8,56,512]{2,1,0:T(8,128)(2,1)S(1)}, u32[]{:S(2)}, u32[]{:S(2)}) async-start(bf16[8,56,512]{2,1,0:T(8,128)(2,1)} %broadcast_in_dim.15), calls=%async_computation.1 | async-start | bytes 917504 | tf_op jit(solution)/shard_map/all_to_all | solution.py:43
  33.0 7.4 %collective-permute-start = (bf16[2,112,384]{2,1,0:T(8,128)(2,1)S(1)}, bf16[2,112,384]{2,1,0:T(8,128)(2,1)S(1)}, u32[]{:S(2)}, u32[]{:S(2)}) collective-permute-start(bf16[2,112,384]{2,1,0:T(8,128)(2,1)S(1)} %pad_maximum_fusion.3.refs_1_), channel_id=1, source_target_pairs={{0,8},{2,10},{4,12},{6,14},{8,0},{10,2},{12,4},{14,6},{1,9},{3,11}... | collective-permute-start | bytes 516104 | tf_op jit(solution)/shard_map/ppermute | solution.py:39
  40.4 2.4 %collective-permute-start.1 = (bf16[2,112,384]{2,1,0:T(8,128)(2,1)S(1)}, bf16[2,112,384]{2,1,0:T(8,128)(2,1)S(1)}, u32[]{:S(2)}, u32[]{:S(2)}) collective-permute-start(bf16[2,112,384]{2,1,0:T(8,128)(2,1)S(1)} %pad_maximum_fusion.3.refs_1_), channel_id=1, source_target_pairs={{0,4},{2,6},{4,8},{6,10},{8,12},{10,14},{12,0},{14,2},{1,5},{3,7},... | collective-permute-start | bytes 516104 | tf_op jit(solution)/shard_map/ppermute | solution.py:39
  42.9 5.0 %collective-permute-start.2 = (bf16[2,112,384]{2,1,0:T(8,128)(2,1)S(1)}, bf16[2,112,384]{2,1,0:T(8,128)(2,1)S(1)}, u32[]{:S(2)}, u32[]{:S(2)}) collective-permute-start(bf16[2,112,384]{2,1,0:T(8,128)(2,1)S(1)} %pad_maximum_fusion.3.refs_1_), channel_id=1, source_target_pairs={{0,12},{2,14},{4,0},{6,2},{8,4},{10,6},{12,8},{14,10},{1,13},{3,15... | collective-permute-start | bytes 516104 | tf_op jit(solution)/shard_map/ppermute | solution.py:39
  47.8 3.8 %collective-permute-done.1.refs_3_ = bf16[2,112,384]{2,1,0:T(8,128)(2,1)S(1)} collective-permute-done((bf16[2,112,384]{2,1,0:T(8,128)(2,1)S(1)}, bf16[2,112,384]{2,1,0:T(8,128)(2,1)S(1)}, u32[]{:S(2)}, u32[]{:S(2)}) %collective-permute-start.1) | collective-permute-done | bytes 172064 | tf_op jit(solution)/shard_map/ppermute | solution.py:39
  51.6 5.2 %collective-permute-done.2.refs_4_ = bf16[2,112,384]{2,1,0:T(8,128)(2,1)S(1)} collective-permute-done((bf16[2,112,384]{2,1,0:T(8,128)(2,1)S(1)}, bf16[2,112,384]{2,1,0:T(8,128)(2,1)S(1)}, u32[]{:S(2)}, u32[]{:S(2)}) %collective-permute-start.2) | collective-permute-done | bytes 172064 | tf_op jit(solution)/shard_map/ppermute | solution.py:39
  56.9 2.7 %collective-permute-start.3 = (bf16[2,2,112,384]{3,2,1,0:T(8,128)(2,1)S(1)}, bf16[2,2,112,384]{3,2,1,0:T(8,128)(2,1)S(1)}, u32[]{:S(2)}, u32[]{:S(2)}) collective-permute-start(bf16[2,2,112,384]{3,2,1,0:T(8,128)(2,1)S(1)} %pad_maximum_fusion.2), channel_id=1, source_target_pairs={{0,2},{2,4},{4,6},{6,8},{8,10},{10,12},{12,14},{14,0},{1,3},{3,5},... | collective-permute-start | bytes 1032200 | tf_op jit(solution)/shard_map/ppermute | solution.py:39
  59.6 3.8 %collective-permute-start.4 = (bf16[2,2,112,384]{3,2,1,0:T(8,128)(2,1)S(1)}, bf16[2,2,112,384]{3,2,1,0:T(8,128)(2,1)S(1)}, u32[]{:S(2)}, u32[]{:S(2)}) collective-permute-start(bf16[2,2,112,384]{3,2,1,0:T(8,128)(2,1)S(1)} %pad_maximum_fusion.2), channel_id=1, source_target_pairs={{0,14},{2,0},{4,2},{6,4},{8,6},{10,8},{12,10},{14,12},{1,15},{3,1}... | collective-permute-start | bytes 1032200 | tf_op jit(solution)/shard_map/ppermute | solution.py:39
  63.4 5.3 %collective-permute-done.3.refs_5_ = bf16[2,2,112,384]{3,2,1,0:T(8,128)(2,1)S(1)} collective-permute-done((bf16[2,2,112,384]{3,2,1,0:T(8,128)(2,1)S(1)}, bf16[2,2,112,384]{3,2,1,0:T(8,128)(2,1)S(1)}, u32[]{:S(2)}, u32[]{:S(2)}) %collective-permute-start.3) | collective-permute-done | bytes 344096 | tf_op jit(solution)/shard_map/ppermute | solution.py:39
  68.7 1.6 collective-permute-done.4.refs_6_
  70.4 3.5 %collective-permute-start.5 = (bf16[8,2,112,384]{3,2,1,0:T(8,128)(2,1)S(1)}, bf16[8,2,112,384]{3,2,1,0:T(8,128)(2,1)}, u32[]{:S(2)}, u32[]{:S(2)}) collective-permute-start(bf16[8,2,112,384]{3,2,1,0:T(8,128)(2,1)S(1)} %place.1), channel_id=1, source_target_pairs={{0,1},{1,0},{2,3},{3,2},{4,5},{5,4},{6,7},{7,6},{8,9},{9,8},{10,11... | collective-permute-start | bytes 4128776 | tf_op jit(solution)/shard_map/ppermute | solution.py:39
  74.0 2.1 %fusion.4 = f32[24,512]{1,0:T(8,128)S(1)} fusion(bf16[1,512,1792]{2,1,0:T(8,128)(2,1)} %param.12, bf16[8,1792]{1,0:T(8,128)(2,1)S(1)} %get-tuple-element.46, bf16[8,1792]{1,0:T(8,128)(2,1)S(1)} %get-tuple-element.47, bf16[8,1792]{1,0:T(8,128)(2,1)S(1)} %get-tuple-element.45), kind=kOutput, calls=%fused_computation.5 | convolution fusion | flops 44298240 | bytes 1970176 | tf_op jit(solution)/shard_map/dot_general | solution.py:32
  76.1 1.4 broadcast_in_dim.16
  77.5 4.4 %all-to-all-start.2 = ((bf16[4,448,512]{2,1,0:T(8,128)(2,1)}), bf16[4,448,512]{2,1,0:T(8,128)(2,1)}, u32[]{:S(2)}, u32[]{:S(2)}) async-start(bf16[4,448,512]{2,1,0:T(8,128)(2,1)} %broadcast_in_dim.16), calls=%async_computation.2 | async-start | bytes 3670016 | tf_op jit(solution)/shard_map/all_to_all | solution.py:43
  81.9 1.6 broadcast_select_fusion.1
  84.0 0.3 fusion.22
  84.3 1.3 pad_maximum_fusion
  85.6 4.5 %fusion.55 = f32[1024,384]{1,0:T(8,128)S(1)} fusion(bf16[1792,1024]{1,0:T(8,128)(2,1)} %all-gather.2.cloned.1.call-done, bf16[1792,384]{1,0:T(8,128)(2,1)} %bitcast.60), kind=kOutput, calls=%fused_computation.92 | convolution fusion | flops 1409286144 | bytes 6619136 | tf_op jit(solution)/shard_map/dot_general | solution.py:32
  90.1 0.3 multiply_convert_fusion.1
  90.4 15.2 %all-to-all-done.2 = bf16[4,448,512]{2,1,0:T(8,128)(2,1)} async-done(((bf16[4,448,512]{2,1,0:T(8,128)(2,1)}), bf16[4,448,512]{2,1,0:T(8,128)(2,1)}, u32[]{:S(2)}, u32[]{:S(2)}) %all-to-all-start.2) | async-done | bytes 1835040 | tf_op jit(solution)/shard_map/all_to_all | solution.py:43
  105.9 0.9 broadcast_in_dim.17
  106.8 7.8 %all-to-all-start.3 = ((f32[32,8,512]{2,1,0:T(8,128)}), f32[32,8,512]{2,1,0:T(8,128)}, u32[]{:S(2)}, u32[]{:S(2)}) async-start(f32[32,8,512]{2,1,0:T(8,128)} %broadcast_in_dim.17), calls=%async_computation.4 | async-start | bytes 1048576 | tf_op jit(solution)/shard_map/all_to_all | solution.py:43
  114.6 1.7 copy.11
  116.3 1.5 fusion.12
  117.8 0.5 copy-done.9
  118.3 3.6 %fusion.13._ = f32[1792,384]{1,0:T(8,128)} fusion(bf16[1792,1024]{1,0:T(8,128)(2,1)S(1)} %copy-done.9, bf16[512,384]{1,0:T(8,128)(2,1)S(1)} %get-tuple-element.40, bf16[512,384]{1,0:T(8,128)(2,1)S(1)} %get-tuple-element.39), kind=kOutput, calls=%fused_computation.20 | convolution fusion | flops 1410859008 | bytes 7208960 | tf_op jit(solution)/shard_map/dot_general | solution.py:32
  122.0 8.1 %all-to-all-done.3 = f32[32,8,512]{2,1,0:T(8,128)} async-done(((f32[32,8,512]{2,1,0:T(8,128)}), f32[32,8,512]{2,1,0:T(8,128)}, u32[]{:S(2)}, u32[]{:S(2)}) %all-to-all-start.3) | async-done | bytes 524320 | tf_op jit(solution)/shard_map/all_to_all | solution.py:43
  130.1 1.1 reduce_sum.27.p_sum
  131.2 1.2 fusion.43
  132.4 0.4 fusion.2
  132.8 0.6 fusion.29
  133.4 16.6 %all_to_all.35 = f32[16,8,128]{2,1,0:T(8,128)S(1)} all-to-all(f32[16,8,128]{2,1,0:T(8,128)S(1)} %concatenate.30), channel_id=1, replica_groups=mesh['z'=8,'x'=4,'y'=8,'c'=2] {'y','c'}, dimensions={0} | all-to-all | bytes 131072 | tf_op jit(solution)/shard_map/all_to_all | solution.py:43
  150.0 0.7 broadcast_in_dim.18
  150.7 4.4 %all-to-all-start.5 = ((f32[32,8,128]{2,1,0:T(8,128)}), f32[32,8,128]{2,1,0:T(8,128)S(1)}, u32[]{:S(2)}, u32[]{:S(2)}) async-start(f32[32,8,128]{2,1,0:T(8,128)} %broadcast_in_dim.18), calls=%async_computation.6 | async-start | bytes 262144 | tf_op jit(solution)/shard_map/all_to_all | solution.py:43
  155.1 2.1 %triangle.1 = f32[8,128]{1,0:T(8,128)} custom-call(f32[8,512]{1,0:T(8,128)} %copy-done.4, f32[1792,384]{1,0:T(8,128)} %fusion.13._), custom_call_target="tpu_custom_call" | custom-call | tf_op jit(solution)/shard_map/triangle/pallas_call | solution.py:115
  157.2 7.6 %all-to-all-done.5 = f32[32,8,128]{2,1,0:T(8,128)S(1)} async-done(((f32[32,8,128]{2,1,0:T(8,128)}), f32[32,8,128]{2,1,0:T(8,128)S(1)}, u32[]{:S(2)}, u32[]{:S(2)}) %all-to-all-start.5) | async-done | bytes 131104 | tf_op jit(solution)/shard_map/all_to_all | solution.py:43
  164.9 0.7 pad_maximum_fusion.11
  165.6 14.5 %all_to_all.36.parts = f32[16,8,256]{2,1,0:T(8,128)} all-to-all(f32[16,8,256]{2,1,0:T(8,128)S(1)} %broadcast_in_dim.19), channel_id=1, replica_groups=mesh['z'=8,'x'=4,'y'=8,'c'=2] {'y','c'}, dimensions={0} | all-to-all | bytes 262144 | tf_op jit(solution)/shard_map/all_to_all | solution.py:43
  180.1 2.6 %finish.1 = (f32[8,1792]{1,0:T(8,128)}, bf16[6,8,512]{2,1,0:T(8,128)(2,1)}, bf16[6,8,1792]{2,1,0:T(8,128)(2,1)}) custom-call(f32[16,8,256]{2,1,0:T(8,128)} %all_to_all.36.parts, f32[8,512]{1,0:T(8,128)} %copy-done.4), custom_call_target="tpu_custom_call" | custom-call | flops 40000000000 | bytes 130000000 | tf_op jit(solution)/shard_map/finish/pallas_call | solution.py:169
  182.7 1.7 fusion.56
  184.4 2.4 %fusion.1 = bf16[1,512,1792]{2,1,0:T(8,128)(2,1)} fusion(f32[512,1792,1]{1,0,2:T(8,128)S(1)} %fusion.56, bf16[512,384]{1,0:T(8,128)(2,1)S(1)} %copy-done.2, bf16[1792,384]{1,0:T(8,128)(2,1)S(1)} %bitcast.56, bf16[1,512,1792]{2,1,0:T(8,128)(2,1)S(1)} %copy-done), kind=kOutput, calls=%fused_computation.2 | convolution fusion | flops 708313088 | bytes 9109504 | tf_op jit(solution)/shard_map/dot_general | solution.py:32
  186.8 1.6 convert_bitcast_fusion
  (45 shorter events, 1.2 us)
Async XLA Ops:
  7.2 6.6 %copy-start.5 = (bf16[384,112]{0,1:T(8,128)(2,1)S(1)}, bf16[384,112]{0,1:T(8,128)(2,1)}, u32[]{:S(2)}) copy-start(bf16[384,112]{0,1:T(8,128)(2,1)} %param.8) | copy-start | bytes 258052
  7.2 6.6 %copy-start.6 = (bf16[384,112]{0,1:T(8,128)(2,1)S(1)}, bf16[384,112]{0,1:T(8,128)(2,1)}, u32[]{:S(2)}) copy-start(bf16[384,112]{0,1:T(8,128)(2,1)} %param.7) | copy-start | bytes 258052
  7.2 14.0 %copy-start.8 = (bf16[512,56]{0,1:T(8,128)(2,1)S(1)}, bf16[512,56]{0,1:T(8,128)(2,1)}, u32[]{:S(2)}) copy-start(bf16[512,56]{0,1:T(8,128)(2,1)} %param.11) | copy-start | bytes 172036
  8.9 11.4 %all-to-all-start = ((bf16[4,56,1024]{2,1,0:T(8,128)(2,1)}), bf16[4,56,1024]{2,1,0:T(8,128)(2,1)S(1)}, u32[]{:S(2)}, u32[]{:S(2)}) async-start(bf16[4,56,1024]{2,1,0:T(8,128)(2,1)} %broadcast_in_dim.14), calls=%async_computation | async-start | bytes 917504 | tf_op jit(solution)/shard_map/all_to_all | solution.py:43
  13.8 71.8 %all-gather.2.cloned.1.call-start = ((), (), s32[]{:S(2)}) async-start(), calls=%async_computation.8 | async-start | bytes 4128768 | tf_op jit(solution)/shard_map/all_gather | solution.py:204
  20.3 0.8 copy-start.3
  22.0 34.9 %all-to-all-start.1 = ((bf16[8,56,512]{2,1,0:T(8,128)(2,1)}), bf16[8,56,512]{2,1,0:T(8,128)(2,1)S(1)}, u32[]{:S(2)}, u32[]{:S(2)}) async-start(bf16[8,56,512]{2,1,0:T(8,128)(2,1)} %broadcast_in_dim.15), calls=%async_computation.1 | async-start | bytes 917504 | tf_op jit(solution)/shard_map/all_to_all | solution.py:43
  33.0 14.9 %collective-permute-start = (bf16[2,112,384]{2,1,0:T(8,128)(2,1)S(1)}, bf16[2,112,384]{2,1,0:T(8,128)(2,1)S(1)}, u32[]{:S(2)}, u32[]{:S(2)}) collective-permute-start(bf16[2,112,384]{2,1,0:T(8,128)(2,1)S(1)} %pad_maximum_fusion.3.refs_1_), channel_id=1, source_target_pairs={{0,8},{2,10},{4,12},{6,14},{8,0},{10,2},{12,4},{14,6},{1,9},{3,11}... | collective-permute-start | bytes 516104 | tf_op jit(solution)/shard_map/ppermute | solution.py:39
  40.4 11.2 %collective-permute-start.1 = (bf16[2,112,384]{2,1,0:T(8,128)(2,1)S(1)}, bf16[2,112,384]{2,1,0:T(8,128)(2,1)S(1)}, u32[]{:S(2)}, u32[]{:S(2)}) collective-permute-start(bf16[2,112,384]{2,1,0:T(8,128)(2,1)S(1)} %pad_maximum_fusion.3.refs_1_), channel_id=1, source_target_pairs={{0,4},{2,6},{4,8},{6,10},{8,12},{10,14},{12,0},{14,2},{1,5},{3,7},... | collective-permute-start | bytes 516104 | tf_op jit(solution)/shard_map/ppermute | solution.py:39
  42.9 14.0 %collective-permute-start.2 = (bf16[2,112,384]{2,1,0:T(8,128)(2,1)S(1)}, bf16[2,112,384]{2,1,0:T(8,128)(2,1)S(1)}, u32[]{:S(2)}, u32[]{:S(2)}) collective-permute-start(bf16[2,112,384]{2,1,0:T(8,128)(2,1)S(1)} %pad_maximum_fusion.3.refs_1_), channel_id=1, source_target_pairs={{0,12},{2,14},{4,0},{6,2},{8,4},{10,6},{12,8},{14,10},{1,13},{3,15... | collective-permute-start | bytes 516104 | tf_op jit(solution)/shard_map/ppermute | solution.py:39
  56.8 17.1 %copy-start.7 = (f32[8,1792]{1,0:T(8,128)S(1)}, f32[8,1792]{1,0:T(8,128)}, u32[]{:S(2)}) copy-start(f32[8,1792]{1,0:T(8,128)} %param.13) | copy-start | bytes 172036
  56.9 11.8 %collective-permute-start.3 = (bf16[2,2,112,384]{3,2,1,0:T(8,128)(2,1)S(1)}, bf16[2,2,112,384]{3,2,1,0:T(8,128)(2,1)S(1)}, u32[]{:S(2)}, u32[]{:S(2)}) collective-permute-start(bf16[2,2,112,384]{3,2,1,0:T(8,128)(2,1)S(1)} %pad_maximum_fusion.2), channel_id=1, source_target_pairs={{0,2},{2,4},{4,6},{6,8},{8,10},{10,12},{12,14},{14,0},{1,3},{3,5},... | collective-permute-start | bytes 1032200 | tf_op jit(solution)/shard_map/ppermute | solution.py:39
  59.6 10.7 %collective-permute-start.4 = (bf16[2,2,112,384]{3,2,1,0:T(8,128)(2,1)S(1)}, bf16[2,2,112,384]{3,2,1,0:T(8,128)(2,1)S(1)}, u32[]{:S(2)}, u32[]{:S(2)}) collective-permute-start(bf16[2,2,112,384]{3,2,1,0:T(8,128)(2,1)S(1)} %pad_maximum_fusion.2), channel_id=1, source_target_pairs={{0,14},{2,0},{4,2},{6,4},{8,6},{10,8},{12,10},{14,12},{1,15},{3,1}... | collective-permute-start | bytes 1032200 | tf_op jit(solution)/shard_map/ppermute | solution.py:39
  70.4 11.5 %collective-permute-start.5 = (bf16[8,2,112,384]{3,2,1,0:T(8,128)(2,1)S(1)}, bf16[8,2,112,384]{3,2,1,0:T(8,128)(2,1)}, u32[]{:S(2)}, u32[]{:S(2)}) collective-permute-start(bf16[8,2,112,384]{3,2,1,0:T(8,128)(2,1)S(1)} %place.1), channel_id=1, source_target_pairs={{0,1},{1,0},{2,3},{3,2},{4,5},{5,4},{6,7},{7,6},{8,9},{9,8},{10,11... | collective-permute-start | bytes 4128776 | tf_op jit(solution)/shard_map/ppermute | solution.py:39
  77.5 28.1 %all-to-all-start.2 = ((bf16[4,448,512]{2,1,0:T(8,128)(2,1)}), bf16[4,448,512]{2,1,0:T(8,128)(2,1)}, u32[]{:S(2)}, u32[]{:S(2)}) async-start(bf16[4,448,512]{2,1,0:T(8,128)(2,1)} %broadcast_in_dim.16), calls=%async_computation.2 | async-start | bytes 3670016 | tf_op jit(solution)/shard_map/all_to_all | solution.py:43
  90.4 25.8 %copy-start.1 = (bf16[512,384]{1,0:T(8,128)(2,1)}, bf16[512,384]{1,0:T(8,128)(2,1)S(1)}, u32[]{:S(2)}) copy-start(bf16[512,384]{1,0:T(8,128)(2,1)S(1)} %multiply_convert_fusion.1) | copy-start | bytes 1179652
  106.8 23.3 %all-to-all-start.3 = ((f32[32,8,512]{2,1,0:T(8,128)}), f32[32,8,512]{2,1,0:T(8,128)}, u32[]{:S(2)}, u32[]{:S(2)}) async-start(f32[32,8,512]{2,1,0:T(8,128)} %broadcast_in_dim.17), calls=%async_computation.4 | async-start | bytes 1048576 | tf_op jit(solution)/shard_map/all_to_all | solution.py:43
  114.5 72.3 %reduce-scatter.2.cloned.1.call-start = ((), (), s32[]{:S(2)}) async-start(), calls=%async_computation.9 | async-start | bytes 2924544 | tf_op jit(solution)/shard_map/reduce_scatter | solution.py:261
  116.3 2.0 %copy-start.9 = (bf16[1792,1024]{1,0:T(8,128)(2,1)S(1)}, bf16[1792,1024]{1,0:T(8,128)(2,1)}, u32[]{:S(2)}) copy-start(bf16[1792,1024]{1,0:T(8,128)(2,1)} %all-gather.2.cloned.1.call-done) | copy-start | bytes 11010052
  122.0 10.4 %copy-start = (bf16[1,512,1792]{2,1,0:T(8,128)(2,1)S(1)}, bf16[1,512,1792]{2,1,0:T(8,128)(2,1)}, u32[]{:S(2)}) copy-start(bf16[1,512,1792]{2,1,0:T(8,128)(2,1)} %param.12) | copy-start | bytes 5505028
  131.2 2.2 %copy-start.4 = (f32[8,512]{1,0:T(8,128)}, f32[8,512]{1,0:T(8,128)S(1)}, u32[]{:S(2)}) copy-start(f32[8,512]{1,0:T(8,128)S(1)} %reduce_sum.27.p_sum) | copy-start | bytes 49156
  150.7 14.2 %all-to-all-start.5 = ((f32[32,8,128]{2,1,0:T(8,128)}), f32[32,8,128]{2,1,0:T(8,128)S(1)}, u32[]{:S(2)}, u32[]{:S(2)}) async-start(f32[32,8,128]{2,1,0:T(8,128)} %broadcast_in_dim.18), calls=%async_computation.6 | async-start | bytes 262144 | tf_op jit(solution)/shard_map/all_to_all | solution.py:43
  182.7 1.7 copy-start.2
Sparse Core Ops, SparseCore 0:
  21.3 60.6 all-gather.1
  122.1 63.2 reduce-scatter.1
